TPU v7x, 128 devices: a whole 4x4x4 slice. The times are simulated.
128 devices in a mesh: ctx: 16 (over x, z), ffn: 8 (over y, core).
Axes of the slice: x: 4, y: 4, z: 4, core: 2. Of those that a mesh axis runs over, the one named last changes fastest.
Arguments:
- queries: bfloat16 [64, 8192], P('ffn'), may hold values from -12 to 12
- key_cache: bfloat16 [64, 2048, 512], P('ffn', 'ctx'), may hold values from -12 to 12
- value_cache: bfloat16 [64, 2048, 512], P('ffn', 'ctx'), may hold values from -6 to 6
- lengths: int32 [64], P('ffn'), may hold values from 1 to 2048, as said below
- residual: bfloat16 [64, 4096], P('ffn', 'ctx'), may hold values from -24 to 24
- o_weight: bfloat16 [8192, 4096], P('ctx'), may hold values from -0.59765625 to 0.59765625
- norm_gain: float32 [4096], P('ctx'), may hold values from 0.1 to 1.9
- gate_proj: bfloat16 [64, 4096, 1536], P('ffn', 'ctx'), may hold values from -0.09375 to 0.09375
- up_proj: bfloat16 [64, 4096, 1536], P('ffn', 'ctx'), may hold values from -0.09375 to 0.09375
- down_proj: bfloat16 [64, 1536, 4096], P('ffn', None, 'ctx'), may hold values from -0.15625 to 0.15625
- expert_ids: int32 [64, 8], P('ffn'), may hold values from 0 to 63, all different within a row; in each aligned block of 8 rows (0 to 7, 8 to 15, ...) at most 2 rows name the same one
- route_weight: float32 [64, 8], P('ffn'), may hold values from 0.05 to 0.3
Outputs:
- moe_out: bfloat16 [64, 4096], P('ffn', 'ctx')
Inputs may be any that keep to these rules, and one draw needn't show every extreme that they name: `lengths`: some request has all 2048 positions filled. `expert_ids`: the 8 experts of a token differ; among the 8 tokens of one index of ffn, no expert is chosen more than 2 times, a bound that some block reaches.
All inputs are finite; a program needn't handle non-finite values.
Results may differ from a plain program's by a relative error of at most 0.035.
Values may be sent and summed in bfloat16 or wider, within the bound.
A program may use at most 128 MiB of HBM per device.

v0:
```python
import jax
import jax.numpy as jnp
from jax import lax
from jax.sharding import PartitionSpec as P

D = 4096
HQ = 64
KVH = 4
HD = 128
MOST = 2


def local(
    queries,
    key_cache,
    value_cache,
    lengths,
    residual,
    o_weight,
    norm_gain,
    gate_proj,
    up_proj,
    down_proj,
    expert_ids,
    route_weight,
):
    ctx_count = lax.axis_size("ctx")
    ctx_place = lax.axis_index("ctx")
    ffn_count = lax.axis_size("ffn")
    requests = queries.shape[0]
    context = key_cache.shape[1]
    group = HQ // KVH
    query_heads = queries.reshape(requests, KVH, group, HD)
    key_heads = key_cache.reshape(requests, context, KVH, HD)
    value_heads = value_cache.reshape(requests, context, KVH, HD)
    scores = jnp.einsum(
        "rkgd,rckd->rkgc", query_heads, key_heads, preferred_element_type=jnp.float32
    ) * HD ** (-0.5)
    position = ctx_place * context + jnp.arange(context, dtype=jnp.int32)
    usable = (position[None, :] < lengths[:, None])[:, None, None, :]
    masked = jnp.where(usable, scores, -1e30)
    peak_score = lax.pmax(jnp.max(masked, axis=-1, keepdims=True), "ctx")
    probs = jnp.where(usable, jnp.exp(masked - peak_score), 0.0).astype(jnp.bfloat16)
    denominator = jnp.sum(probs.astype(jnp.float32), axis=-1).reshape(requests, HQ)
    numerator = jnp.einsum(
        "rkgc,rckd->rkgd", probs, value_heads, preferred_element_type=jnp.float32
    ).reshape(requests, HQ * HD)
    share = HQ // ctx_count
    numerator_all, denominator_all = lax.psum((numerator, denominator), "ctx")
    numerator_own = lax.dynamic_slice_in_dim(numerator_all, ctx_place * (share * HD), share * HD, 1)
    denominator_own = lax.dynamic_slice_in_dim(denominator_all, ctx_place * share, share, 1)
    attended = (numerator_own.reshape(requests, share, HD) / denominator_own[:, :, None]).astype(
        jnp.bfloat16
    )
    attended = attended.reshape(requests, share * HD)
    projected = jnp.dot(attended, o_weight, preferred_element_type=jnp.float32)
    projected_own = lax.psum_scatter(projected, "ctx", scatter_dimension=1, tiled=True)
    hidden_state = (residual.astype(jnp.float32) + projected_own).astype(jnp.bfloat16)
    hidden_f = hidden_state.astype(jnp.float32)
    square_total = lax.psum(jnp.sum(hidden_f * hidden_f, axis=-1, keepdims=True), "ctx")
    normed = (hidden_f * lax.rsqrt(square_total / D + 1e-06) * norm_gain).astype(jnp.bfloat16)
    local_experts = gate_proj.shape[0]
    experts_all = local_experts * ffn_count
    top_count = expert_ids.shape[1]
    slots_all = experts_all * MOST
    flat_ids = expert_ids.reshape(-1)
    chosen = (flat_ids[:, None] == jnp.arange(experts_all, dtype=jnp.int32)[None, :]).astype(
        jnp.int32
    )
    earlier = jnp.cumsum(chosen, axis=0) - chosen
    ranking = jnp.sum(earlier * chosen, axis=1)
    owner = flat_ids // local_experts
    within = flat_ids % local_experts
    slot_index = within * (ffn_count * MOST) + owner * MOST + ranking
    slot_onehot = (slot_index[:, None] == jnp.arange(slots_all, dtype=jnp.int32)[None, :]).astype(
        jnp.float32
    )
    slot_onehot = slot_onehot.reshape(requests, top_count, slots_all)
    dispatch_map = jnp.sum(slot_onehot, axis=1).astype(jnp.bfloat16)
    outgoing = jnp.einsum(
        "rs,rd->sd", dispatch_map, normed, preferred_element_type=jnp.float32
    ).astype(jnp.bfloat16)
    outgoing = outgoing.reshape(local_experts, ffn_count, MOST, normed.shape[1])
    incoming = lax.all_to_all(outgoing, "ffn", split_axis=1, concat_axis=1, tiled=True)
    expert_rows = incoming.reshape(local_experts, ffn_count * MOST, normed.shape[1])
    gate_part = jnp.einsum(
        "esd,edf->esf", expert_rows, gate_proj, preferred_element_type=jnp.float32
    )
    up_part = jnp.einsum("esd,edf->esf", expert_rows, up_proj, preferred_element_type=jnp.float32)
    gate_full, up_full = (
        lax.psum(gate_part.astype(jnp.bfloat16), "ctx").astype(jnp.float32),
        lax.psum(up_part.astype(jnp.bfloat16), "ctx").astype(jnp.float32),
    )
    inner = (jax.nn.silu(gate_full) * up_full).astype(jnp.bfloat16)
    expert_f = jnp.einsum("esf,efd->esd", inner, down_proj, preferred_element_type=jnp.float32)
    expert_out = expert_f.astype(jnp.bfloat16).reshape(
        local_experts, ffn_count, MOST, down_proj.shape[2]
    )
    returned = lax.all_to_all(expert_out, "ffn", split_axis=1, concat_axis=1, tiled=True).reshape(
        slots_all, down_proj.shape[2]
    )
    combine_map = jnp.sum(slot_onehot * route_weight.reshape(requests, top_count, 1), axis=1)
    mixed = jnp.dot(combine_map, returned.astype(jnp.float32), precision=lax.Precision.HIGHEST)
    return mixed.astype(jnp.bfloat16)


def solution(mesh):
    placed = (
        P("ffn", None),
        P("ffn", "ctx", None),
        P("ffn", "ctx", None),
        P("ffn"),
        P("ffn", "ctx"),
        P("ctx", None),
        P("ctx"),
        P("ffn", "ctx", None),
        P("ffn", "ctx", None),
        P("ffn", None, "ctx"),
        P("ffn", None),
        P("ffn", None),
    )
    return jax.shard_map(
        local, mesh=mesh, in_specs=placed, out_specs=P("ffn", "ctx"), check_vma=False
    )
```

profile of v0, /device:TPU:1, one launch (start us, length us, event | category | flops | bytes accessed | tf_op | source)
XLA Modules:
  0.0 402.7 jit_solution(4978062293003899262)
XLA Ops:
  6.6 0.8 broadcast_compare_fusion
  7.4 0.4 copy-done
  7.8 1.6 fusion.37
  9.4 62.4 %pmax.7 = f32[8,4,16]{2,1,0:T(4,128)S(1)} all-reduce(f32[8,4,16]{2,1,0:T(4,128)S(1)} %get-tuple-element.9), channel_id=1, replica_groups=mesh['ctx'=16,'ffn'=8] {'ctx'}, use_global_device_ids=true, to_apply=%region_5.6 | all-reduce | flops 512 | bytes 4096 | tf_op jit(solution)/shard_map/pmax | solution.py:42
  71.8 1.7 fusion.1
  73.5 0.9 copy.57
  74.4 0.0 reduce-scatter.2.cloned.1.call-start
  74.4 0.8 eq.31
  75.2 0.1 fusion.14
  75.2 0.1 reduce_window_sum.11
  75.3 0.2 select_reduce_fusion.1
  75.5 0.1 reduce_sum.48
  75.6 0.3 convert_reduce_fusion
  75.9 0.1 reshape.124
  76.0 28.5 %psum.36 = f32[8,64]{1,0:T(8,128)S(1)} all-reduce(f32[8,64]{1,0:T(8,128)S(1)} %reshape.124), channel_id=1, replica_groups=mesh['ctx'=16,'ffn'=8] {'ctx'}, use_global_device_ids=true, to_apply=%region_8.9 | all-reduce | flops 512 | bytes 4096 | tf_op jit(solution)/shard_map/psum | solution.py:49
  104.5 0.1 constant_dynamic-slice_fusion
  104.6 0.1 copy.34
  104.6 63.5 %all-reduce.4.cloned.1.call-done = f32[8,8192]{1,0:T(8,128)} async-done(((f32[8,8192]{1,0:T(8,128)}), f32[8,8192]{1,0:T(8,128)}) %all-reduce.4.cloned.1.call-update) | async-done | bytes 262160 | tf_op jit(solution)/shard_map/psum | solution.py:49
  168.1 3.6 fusion.19
  171.7 0.0 all-reduce.6.cloned.1.call-start
  171.8 0.1 convert_reduce_fusion.1
  171.9 70.6 %reduce-scatter.2.cloned.1.call-done = f32[8,256]{1,0:T(8,128)} async-done(((f32[8,4096]{1,0:T(8,128)}), f32[8,256]{1,0:T(8,128)}) %reduce-scatter.2.cloned.1.call-update) | async-done | bytes 8208 | tf_op jit(solution)/shard_map/reduce_scatter | solution.py:57
  242.6 0.8 fusion.16
  243.4 30.9 %psum.37 = f32[8,1]{0,1:T(1,128)S(1)} all-reduce(f32[8,1]{0,1:T(1,128)S(1)} %bitcast.44), channel_id=1, replica_groups=mesh['ctx'=16,'ffn'=8] {'ctx'}, use_global_device_ids=true, to_apply=%region_11.12 | all-reduce | flops 8 | bytes 64 | tf_op jit(solution)/shard_map/psum | solution.py:60
  274.3 1.0 convolution_convert_fusion.3
  275.4 18.7 %all_to_all.10 = bf16[8,8,2,256]{3,2,0,1:T(2,128)(2,1)S(1)} all-to-all(bf16[8,8,2,256]{3,2,0,1:T(2,128)(2,1)S(1)} %copy.35), channel_id=1, replica_groups=mesh['ctx'=16,'ffn'=8] {'ffn'}, dimensions={1} | all-to-all | bytes 131072 | tf_op jit(solution)/shard_map/all_to_all | solution.py:84
  294.2 4.6 %convolution_convert_fusion = bf16[8,16,1536]{2,1,0:T(8,128)(2,1)} fusion(bf16[8,16,256]{2,1,0:T(8,128)(2,1)S(1)} %reshape.126, bf16[8,256,1536]{2,1,0:T(8,128)(2,1)} %param.20), kind=kOutput, calls=%fused_computation | convolution fusion | flops 100859904 | bytes 6750208 | tf_op jit(solution)/shard_map/esd,edf->esf/dot_general | solution.py:89
  298.8 1.7 convolution_convert_fusion.1
  300.6 79.7 %all-reduce.6.cloned.1.call-done = (bf16[8,16,1536]{2,1,0:T(8,128)(2,1)}, bf16[8,16,1536]{2,1,0:T(8,128)(2,1)}) async-done(((bf16[8,16,1536]{2,1,0:T(8,128)(2,1)}, bf16[8,16,1536]{2,1,0:T(8,128)(2,1)}), (bf16[8,16,1536]{2,1,0:T(8,128)(2,1)}, bf16[8,16,1536]{2,1,0:T(8,128)(2,1)})) %all-reduce.6.cloned.1.call-update) | async-done | bytes 786448 | tf_op jit(solution)/shard_map/psum | solution.py:92
  380.2 4.0 convolution_convert_fusion.2
  384.3 11.0 %all_to_all.11 = bf16[8,8,2,256]{3,2,0,1:T(2,128)(2,1)S(1)} all-to-all(bf16[8,8,2,256]{3,2,0,1:T(2,128)(2,1)S(1)} %copy.37), channel_id=1, replica_groups=mesh['ctx'=16,'ffn'=8] {'ffn'}, dimensions={1} | all-to-all | bytes 131072 | tf_op jit(solution)/shard_map/all_to_all | solution.py:99
  395.4 0.7 convolution_convert_fusion.4
  (29 shorter events, 0.5 us)
Async XLA Ops:
  6.5 1.2 copy-start
  6.5 165.2 %copy-start.2 = (s32[8,8]{1,0:T(8,128)S(1)}, s32[8,8]{1,0:T(8,128)}, u32[]{:S(2)}) copy-start(s32[8,8]{1,0:T(8,128)} %param.22) | copy-start | bytes 772
  6.5 165.3 %copy-start.3 = (f32[8,8]{1,0:T(8,128)S(1)}, f32[8,8]{1,0:T(8,128)}, u32[]{:S(2)}) copy-start(f32[8,8]{1,0:T(8,128)} %param.23) | copy-start | bytes 772
  6.5 236.0 %copy-start.1 = (bf16[8,256]{1,0:T(8,128)(2,1)S(1)}, bf16[8,256]{1,0:T(8,128)(2,1)}, u32[]{:S(2)}) copy-start(bf16[8,256]{1,0:T(8,128)(2,1)} %param.16) | copy-start | bytes 12292
  6.5 267.8 %copy-start.4 = (f32[256]{0:T(256)S(1)}, f32[256]{0:T(256)}, u32[]{:S(2)}) copy-start(f32[256]{0:T(256)} %param.18) | copy-start | bytes 3076
  6.5 161.6 %all-reduce.4.cloned.1.call-start = ((), (), s32[]{:S(2)}) async-start(), calls=%async_computation.3 | async-start | bytes 524288 | tf_op jit(solution)/shard_map/psum | solution.py:49
  74.4 168.2 %reduce-scatter.2.cloned.1.call-start = ((), (), s32[]{:S(2)}) async-start(), calls=%async_computation.4 | async-start | bytes 139264 | tf_op jit(solution)/shard_map/reduce_scatter | solution.py:57
  171.7 208.5 %all-reduce.6.cloned.1.call-start = ((), (), s32[]{:S(2)}) async-start(), calls=%async_computation.5 | async-start | bytes 1572864 | tf_op jit(solution)/shard_map/psum | solution.py:92
  171.8 127.0 %slice-start = ((s8[6291456]{0:T(1024)(128)(4,1)}), s8[2097152]{0:T(1024)(128)(4,1)S(1)}, s32[]{:S(2)}) async-start(s8[6291456]{0:T(1024)(128)(4,1)} %bitcast.39), calls=%async_computation.6 | async-start | bytes 4194304
  294.2 4.6 %slice-start.1 = ((s8[6291456]{0:T(1024)(128)(4,1)}), s8[4194304]{0:T(1024)(128)(4,1)S(1)}, s32[]{:S(2)}) async-start(s8[6291456]{0:T(1024)(128)(4,1)} %bitcast.39), calls=%async_computation.7 | async-start | bytes 8388608
Sparse Core Ops, SparseCore 0:
  74.5 93.6 all-reduce.3
  171.8 70.6 reduce-scatter.1
  300.7 79.4 all-reduce.5
where the time goes:
time: 403 us
  waiting for transfers between devices  214 us (53%)
  blocking collectives  152 us (38%)
  matrix products  18.9 us (5%)
  between operations  13.2 us (3%)
    psum x1, waiting for transfers between devices, local(): lax.psum(up_part.astype(jnp.bfloat16), 'ctx').astype(jnp.float32)  79.7 us
    reduce_scatter x1, waiting for transfers between devices, local(): lax.psum_scatter(projected, 'ctx', scatter_dimension=1, tiled=True)  70.6 us
    psum x1, waiting for transfers between devices, local(): numerator_all, denominator_all = lax.psum((numerator, denominator), 'ctx')  63.5 us
    pmax x1, blocking collectives, local(): peak_score = lax.pmax(jnp.max(masked, axis=-1, keepdims=True), 'ctx')  62.4 us
    psum x1, blocking collectives, local(): lax.psum(jnp.sum(hidden_f * hidden_f, axis=-1, keepdims=True), 'ctx')  30.9 us
    psum x1, blocking collectives, local(): numerator_all, denominator_all = lax.psum((numerator, denominator), 'ctx')  28.5 us
    all_to_all x1, blocking collectives, local(): lax.all_to_all(outgoing, 'ffn', split_axis=1, concat_axis=1, tiled=True)  18.7 us
    all_to_all x1, blocking collectives, local(): lax.all_to_all(expert_out, 'ffn', split_axis=1, concat_axis=1, tiled=True)  11 us
  transfers between devices with their start and end apart: 3, of which 3 were waited for; matrix products, arithmetic and copies ran while one was open for 0% of the time, Pallas kernels for 0%

commit v1 on v0

v1 whole, which is shorter than its diff:
```python
import jax
import jax.numpy as jnp
from jax import lax
from jax.experimental import pallas as pl
from jax.experimental.pallas import tpu as pltpu
from jax.sharding import PartitionSpec as P

D = 4096
HQ = 64
KVH = 4
HD = 128
FFH = 1536
MOST = 2
CTX = 16
SIDE = 4
FFN = 8
R = 8
E_LOC = 8
SLOTS = FFN * MOST
GROUPS = 2
PER = E_LOC // GROUPS
QUARTER = FFH // SIDE
COLS = D // CTX
LOGICAL = pl.DeviceIdType.LOGICAL
F32 = jnp.float32
BF16 = jnp.bfloat16


FAR_FIRST = sorted(
    ((dx, dz) for dx in range(SIDE) for dz in range(SIDE) if (dx, dz) != (0, 0)),
    key=lambda d: -(min(d[0], SIDE - d[0]) + min(d[1], SIDE - d[1])),
)
FFN_FIRST = (4, 5, 3, 2, 6, 7, 1)
OTHERS = (2, 1, 3)
BLOCKS = (2, 1, 3, 0)
HALVES = ((2, 1), (3, 0))


def kernel(
    len_hbm, res_hbm, gain_hbm, ids_hbm, route_hbm,
    q_hbm, k_hbm, v_hbm, o_hbm, g_hbm, u_hbm, d_hbm,
    out,
    lengths, residual, gain, ids, route,
    q_v, k_v, v_v, o_v, gu_v, d_v,
    send_a, recv_a, send_b, recv_b, recv_c, recv_r, recv_s,
    send_1, passing, behind, own_1, recv_1, send_2, recv_2, recv_e, send_f,
    pick, weigh, rows, results, partly,
    in_sem, kv_sem, o_sem, w_sem, send_sem, recv_sem, line_recv,
):
    cx = lax.axis_index("ctx")
    fx = lax.axis_index("ffn")
    sx = cx // SIDE
    sz = lax.rem(cx, SIDE)

    turn_x = [lax.rem(sx + step, SIDE) for step in range(SIDE)]
    turn_z = [lax.rem(sz + step, SIDE) for step in range(SIDE)]
    number_x = [x * (SIDE * FFN) for x in turn_x]
    number_z = [z * FFN + fx for z in turn_z]
    number_f = [cx * FFN + lax.rem(fx + step, FFN) for step in range(FFN)]

    def every_ffn(visit):
        for step in FFN_FIRST:
            visit(number_f[step])

    def place(g):
        return (sx, sz) if g == 0 else (sz, sx)

    def turn(g, step):
        return turn_x[step] if g == 0 else turn_z[step]

    def first_line(g, step):
        return number_x[step] + number_z[0] if g == 0 else number_x[0] + number_z[step]

    def second_line(g, step):
        return first_line(1 - g, step)

    def settle(ref, sem):
        pltpu.make_async_copy(ref, ref, sem).wait()

    def push(src, dst, phase, to, recv=None):
        pltpu.make_async_remote_copy(
            src_ref=src, dst_ref=dst, send_sem=send_sem.at[phase],
            recv_sem=recv_sem.at[phase] if recv is None else recv,
            device_id=to, device_id_type=LOGICAL,
        ).start()

    barrier = pltpu.get_barrier_semaphore()

    def greet(to):
        pl.semaphore_signal(barrier, inc=1, device_id=to, device_id_type=LOGICAL)

    pairs = [
        (q_hbm, q_v), (len_hbm, lengths),
        (ids_hbm, ids), (route_hbm, route), (res_hbm, residual), (gain_hbm, gain),
    ]
    first = [pltpu.make_async_copy(src, dst, in_sem.at[n]) for n, (src, dst) in enumerate(pairs)]
    for copy in first[:4]:
        copy.start()
    kv_copies = []
    for n, step in enumerate(BLOCKS):
        k = turn_x[step]
        span = pl.ds(pl.multiple_of(k * HD, HD), HD)
        kv_copies.append(
            (
                pltpu.make_async_copy(k_hbm.at[:, :, span], k_v.at[n], kv_sem.at[0, n]),
                pltpu.make_async_copy(v_hbm.at[:, :, span], v_v.at[n], kv_sem.at[1, n]),
            )
        )
        for copy in kv_copies[n]:
            copy.start()
    for copy in first[4:]:
        copy.start()
    for dx, dz in FAR_FIRST:
        greet(number_x[dx] + number_z[dz])
    every_ffn(greet)
    o_copies = [
        pltpu.make_async_copy(
            o_hbm.at[pl.ds(n * 128, 128)], o_v.at[pl.ds(n * 128, 128)], o_sem.at[n]
        )
        for n in range(4)
    ]

    for copy in o_copies:
        copy.start()

    def fetch(n, carry):
        for g in range(GROUPS):
            e = g * PER + lax.rem(place(g)[0] + SIDE - 1 - n, SIDE)
            pltpu.make_async_copy(g_hbm.at[e], gu_v.at[e, :, 0:FFH], w_sem.at[0, e]).start()
            pltpu.make_async_copy(u_hbm.at[e], gu_v.at[e, :, FFH:], w_sem.at[1, e]).start()
        return carry

    def fetch_down(e, carry):
        pltpu.make_async_copy(d_hbm.at[e], d_v.at[e], w_sem.at[2, e]).start()
        return carry


    lane8 = lax.broadcasted_iota(jnp.int32, (R, 128), 1)
    sub8 = lax.broadcasted_iota(jnp.int32, (R, 128), 0)
    filled = jnp.zeros((R, 128), jnp.int32)
    row_r = lax.broadcasted_iota(jnp.int32, (128, 128), 0) & 7
    lane_full = lax.broadcasted_iota(jnp.int32, (1, 4, R, 128), 3)
    head4 = lax.broadcasted_iota(jnp.int32, (1, 4, R, 128), 1)
    first[2].wait()
    first[3].wait()
    table = jnp.zeros((R, 128), F32)
    ids_f = ids[...].astype(F32)
    route_f = route[...]
    for k in range(8):
        table = jnp.where(lane8 == k, ids_f[:, k : k + 1], table)
        table = jnp.where(lane8 == 8 + k, route_f[:, k : k + 1], table)
    recv_r[fx] = table
    first[1].wait()
    for r in range(R):
        filled = jnp.where(sub8 == r, lengths[r], filled)
    usable = ((cx * 128 + lane8) < filled)[None]
    first[0].wait()

    def attend(n, k):
        part = q_v[:, pl.ds(pl.multiple_of(k * 16 * HD, 16 * HD), 16 * HD)].astype(F32)
        queries = jnp.concatenate(
            [part[:, g * HD : (g + 1) * HD] for g in range(16)], axis=0
        ).astype(BF16)
        every = lax.dot_general(
            queries, k_v[n].reshape(R * 128, HD), (((1,), (1,)), ((), ())),
            preferred_element_type=F32,
        )
        scores = every[:, 0:128]
        for r in range(1, R):
            scores = jnp.where(row_r == r, every[:, r * 128 : (r + 1) * 128], scores)
        scores = (scores * HD ** (-0.5)).reshape(16, R, 128)
        peak = jnp.max(jnp.where(usable, scores, -1e30), axis=-1, keepdims=True)
        peak = peak.astype(BF16).astype(F32)
        probs = jnp.where(usable, jnp.exp(scores - peak), 0.0)
        probs = probs.astype(BF16).astype(F32)
        total = jnp.sum(probs, axis=-1, keepdims=True)
        flat = probs.reshape(128, 128)
        spread = jnp.concatenate(
            [jnp.where(row_r == r, flat, 0.0).astype(BF16) for r in range(R)], axis=1
        )
        numerator = jnp.dot(spread, v_v[n].reshape(R * 128, HD), preferred_element_type=F32)
        send_a[pl.ds(k * 4, 4), 0:4] = numerator.reshape(4, 4, R, HD).astype(BF16)
        peak4 = jnp.broadcast_to(peak, (16, R, 128)).reshape(4, 4, R, 128)
        total4 = jnp.broadcast_to(total, (16, R, 128)).reshape(4, 4, R, 128)
        high = total4.astype(BF16).astype(F32)
        marks = jnp.sum(
            jnp.where(lane_full == head4, peak4, 0.0)
            + jnp.where(lane_full == head4 + 4, high, 0.0)
            + jnp.where(lane_full == head4 + 8, total4 - high, 0.0),
            axis=1,
        )
        send_a[pl.ds(k * 4, 4), 4] = marks.astype(BF16)

    for n, half in enumerate(HALVES):
        for copy in kv_copies[2 * n] + kv_copies[2 * n + 1]:
            copy.wait()
        for m, step in enumerate(half):
            attend(2 * n + m, turn_x[step])
        if n == 0:
            pl.semaphore_wait(barrier, CTX - 1 + FFN - 1)
            every_ffn(lambda to: push(recv_r.at[fx], recv_r.at[fx], 1, to))
        for step in half:
            for z in OTHERS + ((0,) if step else ()):
                to = turn_x[step] * SIDE + turn_z[z]
                push(send_a.at[to], recv_a.at[cx], 0, number_x[step] + number_z[z])
    recv_a[cx] = send_a[cx]
    lax.fori_loop(0, PER, fetch, 0)
    lax.fori_loop(0, E_LOC, fetch_down, 0)

    settle(recv_r.at[pl.ds(0, FFN - 1)], recv_sem.at[1])
    tables = recv_r[...].reshape(FFN * R, 128)
    lane = lax.broadcasted_iota(jnp.int32, (FFN * R, 128), 1)
    token = lax.broadcasted_iota(jnp.int32, (FFN * R, 128), 0)
    expert = (fx * E_LOC + (lane >> 4)).astype(F32)
    chosen = jnp.zeros((FFN * R, 128), F32)
    weight = jnp.zeros((FFN * R, 128), F32)
    for k in range(8):
        hit = tables[:, k : k + 1] == expert
        chosen = jnp.where(hit, 1.0, chosen)
        weight = jnp.where(hit, tables[:, 8 + k : 9 + k], weight)
    row = lax.broadcasted_iota(jnp.int32, (64, 64), 0)
    col = lax.broadcasted_iota(jnp.int32, (64, 64), 1)
    before = jnp.where((col < row) & ((col >> 3) == (row >> 3)), 1.0, 0.0).astype(BF16)
    rank = jnp.dot(before, chosen.astype(BF16), preferred_element_type=F32)
    here = (
        (chosen > 0.5)
        & (rank == (lane & 1).astype(F32))
        & ((token >> 3) == ((lane & 15) >> 1))
    )
    here_f = jnp.where(here, 1.0, 0.0)
    padded = jnp.concatenate([here_f, jnp.zeros((64, 128), F32)], axis=0)
    pick[...] = jnp.transpose(padded).astype(BF16)
    weight = jnp.where(here, weight, 0.0)
    high = weight.astype(BF16)
    weigh[0:64] = high
    weigh[64:128] = (weight - high.astype(F32)).astype(BF16)

    settle(recv_a.at[pl.ds(0, CTX - 1)], recv_sem.at[0])
    got = recv_a[...].astype(F32)
    marks = got[:, 4]
    factor = jnp.exp(marks - jnp.max(marks, axis=0, keepdims=True))
    share = pltpu.roll(marks, 124, 2) + pltpu.roll(marks, 120, 2)
    below = jnp.sum(factor * share, axis=0)
    heads = []
    for h in range(4):
        top = jnp.zeros((R, HD), F32)
        for c in range(CTX):
            top = top + factor[c, :, h : h + 1] * got[c, h]
        heads.append(top / below[:, h : h + 1])
    attended = jnp.concatenate(heads, axis=1).astype(BF16)

    for copy in o_copies:
        copy.wait()
    for half in HALVES:
        for step in half:
            block = turn_x[step]
            span = pl.ds(pl.multiple_of(block * 1024, 1024), 1024)
            projected = jnp.dot(attended, o_v[:, span], preferred_element_type=F32)
            for z in range(SIDE):
                left, right = projected[:, z * 256 : z * 256 + 128], projected[:, z * 256 + 128 : z * 256 + 256]
                send_b[block * SIDE + z] = jnp.concatenate([left, right], axis=0).astype(BF16)
        for step in half:
            for z in OTHERS + ((0,) if step else ()):
                to = turn_x[step] * SIDE + turn_z[z]
                push(send_b.at[to], recv_b.at[cx], 2, number_x[step] + number_z[z])
    recv_b[cx] = send_b[cx]

    def weights_here(e, carry):
        pltpu.make_async_copy(g_hbm.at[e], gu_v.at[e, :, 0:FFH], w_sem.at[0, e]).wait()
        pltpu.make_async_copy(u_hbm.at[e], gu_v.at[e, :, FFH:], w_sem.at[1, e]).wait()
        return carry

    first[4].wait()
    first[5].wait()
    res = residual[...].astype(F32)
    res = jnp.concatenate([res[:, 0:128], res[:, 128:256]], axis=0)
    settle(recv_b.at[pl.ds(0, CTX - 1)], recv_sem.at[2])
    hidden = res + jnp.sum(recv_b[...].astype(F32), axis=0)
    recv_c[fx] = hidden.astype(BF16)
    every_ffn(lambda to: push(recv_c.at[fx], recv_c.at[fx], 3, to))
    lax.fori_loop(0, E_LOC, weights_here, 0)
    settle(recv_c.at[pl.ds(0, FFN - 1)], recv_sem.at[3])
    tokens = recv_c[...].astype(F32)
    left = tokens[:, 0:8, :].reshape(64, 128)
    right = tokens[:, 8:16, :].reshape(64, 128)
    gained = jnp.concatenate([left * gain[:, 0:128], right * gain[:, 128:256]], axis=1)
    gained = jnp.concatenate([gained, jnp.zeros((64, 256), F32)], axis=0).astype(BF16)
    rows[...] = (
        jnp.dot(pick[...], gained, preferred_element_type=F32)
        .astype(BF16)
        .reshape(E_LOC, SLOTS, COLS)
    )

    def share_squares():
        squares = jnp.sum(left * left + right * right, axis=1, keepdims=True).reshape(FFN, R, 1)
        squares = jnp.broadcast_to(squares, (FFN, R, 128))
        block = lax.broadcasted_iota(jnp.int32, (FFN, R, 128), 0)
        lanes = lax.broadcasted_iota(jnp.int32, (FFN, R, 128), 2)
        recv_s[0, sx] = jnp.sum(jnp.where(lanes == block, squares, 0.0), axis=0)
        for step in OTHERS:
            push(recv_s.at[0, sx], recv_s.at[0, sx], 6, first_line(0, step))

    def gate_up(g, step):
        e = g * PER + turn(g, step)
        both = jnp.dot(rows[e], gu_v[e], preferred_element_type=F32)
        return both[:, 0:FFH], both[:, FFH:]

    for g in range(GROUPS):
        gate, upward = gate_up(g, 2)
        send_1[g, 4] = gate.astype(BF16)
        send_1[g, 5] = upward.astype(BF16)
    for g in range(GROUPS):
        push(send_1.at[g, 5], passing.at[g], 9 + g, first_line(g, 3))
        push(send_1.at[g, 4], recv_1.at[g, 4], 4 + g, first_line(g, 2))
    share_squares()
    for g in range(GROUPS):
        gate, upward = gate_up(g, 1)
        send_1[g, 0] = gate.astype(BF16)
        send_1[g, 1] = upward.astype(BF16)
    for g in range(GROUPS):
        push(send_1.at[g, pl.ds(0, 2)], recv_1.at[g, pl.ds(0, 2)], 4 + g, first_line(g, 1))
    for g in range(GROUPS):
        gate, behind[g] = gate_up(g, 3)
        send_1[g, 2] = gate.astype(BF16)
    for g in range(GROUPS):
        push(send_1.at[g, 2], recv_1.at[g, 2], 4 + g, first_line(g, 3))
    for g in range(GROUPS):
        own_1[g, 0], own_1[g, 1] = gate_up(g, 0)
    for g in range(GROUPS):
        settle(passing.at[g], recv_sem.at[9 + g])
        send_1[g, 3] = (behind[g] + passing[g].astype(F32)).astype(BF16)
        push(send_1.at[g, 3], recv_1.at[g, 3], 4 + g, first_line(g, 3))
    settle(recv_s.at[0, pl.ds(0, SIDE - 1)], recv_sem.at[6])
    recv_s[1, sz] = jnp.sum(recv_s[0], axis=0)
    for step in OTHERS:
        push(recv_s.at[1, sz], recv_s.at[1, sz], 12, second_line(0, step))

    for g in range(GROUPS):
        after = place(g)[1]
        settle(recv_1.at[g], recv_sem.at[4 + g])
        gate = own_1[g, 0]
        upward = own_1[g, 1]
        for c in (0, 2, 4):
            gate = gate + recv_1[g, c].astype(F32)
        for c in (1, 3):
            upward = upward + recv_1[g, c].astype(F32)
        for n in range(SIDE):
            span = slice(n * QUARTER, (n + 1) * QUARTER)
            send_2[g, n, 0:SLOTS] = gate[:, span].astype(BF16)
            send_2[g, n, SLOTS:] = upward[:, span].astype(BF16)
        for step in OTHERS:
            to = turn(1 - g, step)
            push(send_2.at[g, to], recv_2.at[g, after], 7 + g, second_line(g, step))
        recv_2[g, after] = send_2[g, after]

    settle(recv_s.at[1, pl.ds(0, SIDE - 1)], recv_sem.at[12])
    scale = lax.rsqrt(jnp.sum(recv_s[1], axis=0) * (1.0 / D) + 1e-06)
    scale = jnp.concatenate(
        [jnp.broadcast_to(scale[:, b : b + 1], (R, 128)) for b in range(FFN)]
        + [jnp.zeros((64, 128), F32)],
        axis=0,
    )
    high = scale.astype(BF16)
    split = jnp.concatenate([high, (scale - high.astype(F32)).astype(BF16)], axis=1)
    owned = [
        pick[pl.ds(pl.multiple_of((g * PER + place(g)[0]) * SLOTS, SLOTS), SLOTS), :]
        for g in range(GROUPS)
    ]
    scales = jnp.dot(jnp.concatenate(owned, axis=0), split, preferred_element_type=F32)
    scales = scales[:, 0:128] + scales[:, 128:256]
    own_scales = [
        jnp.concatenate([scales[g * SLOTS : (g + 1) * SLOTS]] * (QUARTER // 128), axis=1)
        for g in range(GROUPS)
    ]

    for g in range(GROUPS):
        settle(recv_2.at[g, pl.ds(0, SIDE - 1)], recv_sem.at[7 + g])
        both = recv_2[g, 0].astype(F32)
        for c in range(1, SIDE):
            both = both + recv_2[g, c].astype(F32)
        gate = both[0:SLOTS] * own_scales[g]
        upward = both[SLOTS:] * own_scales[g]
        inner = gate / (1.0 + jnp.exp(-gate)) * upward
        recv_e[sx, sz, g] = inner.astype(BF16)
    for dx, dz in FAR_FIRST:
        push(
            recv_e.at[sx, sz], recv_e.at[sx, sz], 13, number_x[dx] + number_z[dz], line_recv.at[sx]
        )

    def down_here(e, carry):
        pltpu.make_async_copy(d_hbm.at[e], d_v.at[e], w_sem.at[2, e]).wait()
        return carry

    lax.fori_loop(0, E_LOC, down_here, 0)
    for step in (0, 1, 3, 2):
        x = turn_x[step]
        settle(recv_e.at[0, pl.ds(0, SIDE if step else SIDE - 1)], line_recv.at[x])
        inner = jnp.concatenate([recv_e[x, q, 0] for q in range(SIDE)], axis=1)
        results[x] = jnp.dot(inner, d_v[x], preferred_element_type=F32).astype(BF16)
        span = pl.ds(pl.multiple_of(x * QUARTER, QUARTER), QUARTER)
        for n in range(PER):
            term = jnp.dot(recv_e[x, n, 1], d_v[PER + n, span, :], preferred_element_type=F32)
            if step:
                term = term + partly[n]
            if step != 2:
                partly[n] = term
            else:
                results[PER + n] = term.astype(BF16)

    found = results[...].reshape(E_LOC * SLOTS, COLS)
    mixed = jnp.dot(weigh[...], found, preferred_element_type=F32)
    mixed = mixed[0:64] + mixed[64:128]
    for b in range(FFN):
        piece = mixed[b * R : (b + 1) * R]
        send_f[b] = piece.astype(BF16)
    for step in FFN_FIRST:
        push(send_f.at[lax.rem(fx + step, FFN)], out.at[fx], 11, number_f[step])
    kept = pltpu.make_async_copy(send_f.at[fx], out.at[fx], o_sem.at[0])
    kept.start()

    settle(send_a.at[pl.ds(0, CTX - 1)], send_sem.at[0])
    settle(recv_r.at[pl.ds(0, FFN - 1)], send_sem.at[1])
    settle(send_b.at[pl.ds(0, CTX - 1)], send_sem.at[2])
    settle(recv_c.at[pl.ds(0, FFN - 1)], send_sem.at[3])
    settle(recv_s.at[0, pl.ds(0, SIDE - 1)], send_sem.at[6])
    settle(recv_s.at[1, pl.ds(0, SIDE - 1)], send_sem.at[12])
    for g in range(GROUPS):
        settle(recv_1.at[g], send_sem.at[4 + g])
        settle(passing.at[g], send_sem.at[9 + g])
        settle(send_2.at[g, pl.ds(0, SIDE - 1)], send_sem.at[7 + g])
    settle(recv_e.at[pl.ds(0, SIDE - 1)], send_sem.at[13])
    settle(recv_e.at[0, pl.ds(0, SIDE - 1)], send_sem.at[13])
    settle(send_f.at[pl.ds(0, FFN - 1)], send_sem.at[11])

    kept.wait()
    settle(out.at[pl.ds(0, FFN - 1)], recv_sem.at[11])


def local(
    queries, key_cache, value_cache, lengths, residual, o_weight, norm_gain,
    gate_proj, up_proj, down_proj, expert_ids, route_weight,
):
    anywhere = pl.BlockSpec(memory_space=pl.ANY)
    parts = pl.pallas_call(
        kernel,
        out_shape=pltpu.VMEM((FFN, R, COLS), BF16),
        in_specs=[anywhere] * 12,
        out_specs=pl.BlockSpec(memory_space=pltpu.VMEM),
        scratch_shapes=[
            pltpu.SMEM((R,), jnp.int32),
            pltpu.VMEM((R, COLS), BF16),
            pltpu.VMEM((1, COLS), F32),
            pltpu.VMEM((R, 8), jnp.int32),
            pltpu.VMEM((R, 8), F32),
            pltpu.VMEM((R, HQ * HD), BF16),
            pltpu.VMEM((KVH, R, 128, HD), BF16),
            pltpu.VMEM((KVH, R, 128, HD), BF16),
            pltpu.VMEM((HQ * HD // CTX, D), BF16),
            pltpu.VMEM((E_LOC, COLS, 2 * FFH), BF16),
            pltpu.VMEM((E_LOC, FFH, COLS), BF16),
            pltpu.VMEM((CTX, 5, R, 128), BF16),
            pltpu.VMEM((CTX, 5, R, 128), BF16),
            pltpu.VMEM((CTX, 16, 128), BF16),
            pltpu.VMEM((CTX, 16, 128), BF16),
            pltpu.VMEM((FFN, 16, 128), BF16),
            pltpu.VMEM((FFN, R, 128), F32),
            pltpu.VMEM((2, SIDE, R, 128), F32),
            pltpu.VMEM((GROUPS, 6, SLOTS, FFH), BF16),
            pltpu.VMEM((GROUPS, SLOTS, FFH), BF16),
            pltpu.VMEM((GROUPS, SLOTS, FFH), F32),
            pltpu.VMEM((GROUPS, 2, SLOTS, FFH), F32),
            pltpu.VMEM((GROUPS, 5, SLOTS, FFH), BF16),
            pltpu.VMEM((GROUPS, SIDE, 2 * SLOTS, QUARTER), BF16),
            pltpu.VMEM((GROUPS, SIDE, 2 * SLOTS, QUARTER), BF16),
            pltpu.VMEM((SIDE, SIDE, GROUPS, SLOTS, QUARTER), BF16),
            pltpu.VMEM((FFN, R, COLS), BF16),
            pltpu.VMEM((128, 128), BF16),
            pltpu.VMEM((128, 128), BF16),
            pltpu.VMEM((E_LOC, SLOTS, COLS), BF16),
            pltpu.VMEM((E_LOC, SLOTS, COLS), BF16),
            pltpu.VMEM((PER, SLOTS, COLS), F32),
            pltpu.SemaphoreType.DMA((6,)),
            pltpu.SemaphoreType.DMA((2, KVH)),
            pltpu.SemaphoreType.DMA((4,)),
            pltpu.SemaphoreType.DMA((3, E_LOC)),
            pltpu.SemaphoreType.DMA((14,)),
            pltpu.SemaphoreType.DMA((14,)),
            pltpu.SemaphoreType.DMA((SIDE,)),
        ],
        compiler_params=pltpu.CompilerParams(
            collective_id=0, has_side_effects=True, vmem_limit_bytes=56 * 2**20
        ),
        cost_estimate=pl.CostEstimate(
            flops=1_000_000_000, bytes_accessed=26_000_000, transcendentals=100_000
        ),
    )(
        lengths, residual, norm_gain.reshape(1, COLS), expert_ids, route_weight,
        queries, key_cache, value_cache, o_weight, gate_proj, up_proj, down_proj,
    )
    return jnp.sum(parts.astype(F32), axis=0).astype(BF16)


def solution(mesh):
    placed = (
        P("ffn", None),
        P("ffn", "ctx", None),
        P("ffn", "ctx", None),
        P("ffn"),
        P("ffn", "ctx"),
        P("ctx", None),
        P("ctx"),
        P("ffn", "ctx", None),
        P("ffn", "ctx", None),
        P("ffn", None, "ctx"),
        P("ffn", None),
        P("ffn", None),
    )
    return jax.shard_map(
        local, mesh=mesh, in_specs=placed, out_specs=P("ffn", "ctx"), check_vma=False
    )
```

time: 403 us -> 46.1 us (0.11)
  waiting for transfers between devices: 214 us -> 0 us
  blocking collectives: 152 us -> 0 us
  Pallas kernels: 0 us -> 45.4 us
  matrix products: 18.9 us -> 0 us
  between operations: 13.2 us -> 0.01 us
    psum x2 -> x0, waiting for transfers between devices: 143 us -> none  [the longest x1 79.7 us: local(): lax.psum(up_part.astype(jnp.bfloat16), 'ctx').astype(jnp.float32)]
    reduce_scatter x1 -> x0, waiting for transfers between devices: 70.6 us -> none  [local(): lax.psum_scatter(projected, 'ctx', scatter_dimension=1, tiled=True)]
    pmax x1 -> x0, blocking collectives: 62.4 us -> none  [local(): peak_score = lax.pmax(jnp.max(masked, axis=-1, keepdims=True), 'ctx')]
    psum x2 -> x0, blocking collectives: 59.4 us -> none  [the longest x1 30.9 us: local(): lax.psum(jnp.sum(hidden_f * hidden_f, axis=-1, keepdims=True), 'ctx')]
    pallas_call x0 -> x1, Pallas kernels: none -> 45.4 us  [local(): pl.pallas_call(kernel, out_shape=pltpu.VMEM((FFN, R, COLS), BF16), in_spe...]
    all_to_all x2 -> x0, blocking collectives: 29.7 us -> none  [the longest x1 18.7 us: local(): lax.all_to_all(outgoing, 'ffn', split_axis=1, concat_axis=1, tiled=True)]
    dot_general x8 -> x0, matrix products: 18.9 us -> none  [the longest x1 4.62 us: local(): jnp.einsum('esd,edf->esf', expert_rows, up_proj, preferred_element_type=j...]
  transfers between devices with their start and end apart: 3 -> 0, of which waited for: 3 -> 0; matrix products, arithmetic and copies ran while one was open for 0% -> 0% of each run, Pallas kernels for 0% -> 0%
where the time goes in v1:
time: 46.1 us; the launch traced here: 46 us
  Pallas kernels  45.4 us (98%)
  other arithmetic  0.61 us (1%)
    pallas_call x1, Pallas kernels, local(): pl.pallas_call(kernel, out_shape=pltpu.VMEM((FFN, R, COLS), BF16), in_spe...  45.4 us

profile of v1, /device:TPU:1, one launch (start us, length us, event | category | flops | bytes accessed | tf_op | source)
XLA Modules:
  0.0 46.0 jit_solution(9718651903798552095)
XLA Ops:
  0.0 45.4 %shard_map.118 = bf16[8,8,256]{2,1,0:T(8,128)(2,1)S(1)} custom-call(s32[8]{0:T(128)} %len_hbm.1, bf16[8,256]{1,0:T(8,128)(2,1)} %res_hbm.1, f32[1,256]{1,0:T(1,128)} %bitcast.1, s32[8,8]{1,0:T(8,128)} %ids_hbm.1, f32[8,8]{1,0:T(8,128)} %route_hbm.1, bf16[8,8192]{1,0:T(8,128)(2,1)} %q_hbm.1, bf16[8,128,512]{2,1,0:T(8,128)(2,1)} %k_hbm.1, ...), custom_call_target="tpu_custom_call" | custom-call | flops 1000000000 | bytes 26000000 | tf_op jit(solution)/shard_map/pallas_call | solution.py:444
  45.4 0.6 %reduce_sum.12 = bf16[8,256]{1,0:T(8,128)(2,1)} reduce(bf16[8,8,256]{2,1,0:T(8,128)(2,1)S(1)} %shard_map.118, bf16[]{:T(256)} %constant.2.clone.1), dimensions={0}, to_apply=%region_0.0 | reduce | flops 14336 | bytes 36866 | tf_op jit(solution)/shard_map/reduce_sum | solution.py:500

commit v2 on v0

v2 whole, which is shorter than its diff:
```python
import jax
import jax.numpy as jnp
from jax import lax
from jax.experimental import pallas as pl
from jax.experimental.pallas import tpu as pltpu
from jax.sharding import PartitionSpec as P

D = 4096
HQ = 64
KVH = 4
HD = 128
FFH = 1536
MOST = 2
CTX = 16
SIDE = 4
FFN = 8
R = 8
E_LOC = 8
SLOTS = FFN * MOST
GROUPS = 2
PER = E_LOC // GROUPS
QUARTER = FFH // SIDE
COLS = D // CTX
LOGICAL = pl.DeviceIdType.LOGICAL
F32 = jnp.float32
BF16 = jnp.bfloat16


FAR_FIRST = sorted(
    ((dx, dz) for dx in range(SIDE) for dz in range(SIDE) if (dx, dz) != (0, 0)),
    key=lambda d: -(min(d[0], SIDE - d[0]) + min(d[1], SIDE - d[1])),
)
FFN_FIRST = (4, 5, 3, 2, 6, 7, 1)
OTHERS = (2, 1, 3)
BLOCKS = (2, 1, 3, 0)
HALVES = ((2, 1), (3, 0))


def kernel(
    len_hbm, res_hbm, gain_hbm, ids_hbm, route_hbm,
    q_hbm, k_hbm, v_hbm, o_hbm, g_hbm, u_hbm, d_hbm,
    out,
    lengths, residual, gain, ids, route,
    q_v, k_v, v_v, o_v, gu_v, d_v,
    send_a, recv_a, send_b, recv_b, recv_c, recv_r, recv_s,
    send_1, passing, behind, own_1, recv_1, send_2, recv_2, recv_e, send_f,
    pick, weigh, rows, results, partly,
    in_sem, kv_sem, o_sem, w_sem, send_sem, recv_sem, line_recv,
):
    cx = lax.axis_index("ctx")
    fx = lax.axis_index("ffn")
    sx = cx // SIDE
    sz = lax.rem(cx, SIDE)

    turn_x = [lax.rem(sx + step, SIDE) for step in range(SIDE)]
    turn_z = [lax.rem(sz + step, SIDE) for step in range(SIDE)]
    number_x = [x * (SIDE * FFN) for x in turn_x]
    number_z = [z * FFN + fx for z in turn_z]
    number_f = [cx * FFN + lax.rem(fx + step, FFN) for step in range(FFN)]

    def every_ffn(visit):
        for step in FFN_FIRST:
            visit(number_f[step])

    def place(g):
        return (sx, sz) if g == 0 else (sz, sx)

    def turn(g, step):
        return turn_x[step] if g == 0 else turn_z[step]

    def first_line(g, step):
        return number_x[step] + number_z[0] if g == 0 else number_x[0] + number_z[step]

    def second_line(g, step):
        return first_line(1 - g, step)

    def settle(ref, sem):
        pltpu.make_async_copy(ref, ref, sem).wait()

    def push(src, dst, phase, to, recv=None):
        pltpu.make_async_remote_copy(
            src_ref=src, dst_ref=dst, send_sem=send_sem.at[phase],
            recv_sem=recv_sem.at[phase] if recv is None else recv,
            device_id=to, device_id_type=LOGICAL,
        ).start()

    with jax.named_scope("entry"):
        barrier = pltpu.get_barrier_semaphore()

        def greet(to):
            pl.semaphore_signal(barrier, inc=1, device_id=to, device_id_type=LOGICAL)

        pairs = [
            (q_hbm, q_v), (len_hbm, lengths),
            (ids_hbm, ids), (route_hbm, route), (res_hbm, residual), (gain_hbm, gain),
        ]
        first = [pltpu.make_async_copy(src, dst, in_sem.at[n]) for n, (src, dst) in enumerate(pairs)]
        for copy in first[:4]:
            copy.start()
        kv_copies = []
        for n, step in enumerate(BLOCKS):
            k = turn_x[step]
            span = pl.ds(pl.multiple_of(k * HD, HD), HD)
            kv_copies.append(
                (
                    pltpu.make_async_copy(k_hbm.at[:, :, span], k_v.at[n], kv_sem.at[0, n]),
                    pltpu.make_async_copy(v_hbm.at[:, :, span], v_v.at[n], kv_sem.at[1, n]),
                )
            )
            for copy in kv_copies[n]:
                copy.start()
        for copy in first[4:]:
            copy.start()
        for dx, dz in FAR_FIRST:
            greet(number_x[dx] + number_z[dz])
        every_ffn(greet)
        o_copies = [
            pltpu.make_async_copy(
                o_hbm.at[pl.ds(n * 128, 128)], o_v.at[pl.ds(n * 128, 128)], o_sem.at[n]
            )
            for n in range(4)
        ]

        for copy in o_copies:
            copy.start()

        def fetch(n, carry):
            for g in range(GROUPS):
                e = g * PER + lax.rem(place(g)[0] + SIDE - 1 - n, SIDE)
                pltpu.make_async_copy(g_hbm.at[e], gu_v.at[e, :, 0:FFH], w_sem.at[0, e]).start()
                pltpu.make_async_copy(u_hbm.at[e], gu_v.at[e, :, FFH:], w_sem.at[1, e]).start()
            return carry

        def fetch_down(e, carry):
            pltpu.make_async_copy(d_hbm.at[e], d_v.at[e], w_sem.at[2, e]).start()
            return carry


        lane8 = lax.broadcasted_iota(jnp.int32, (R, 128), 1)
        sub8 = lax.broadcasted_iota(jnp.int32, (R, 128), 0)
        filled = jnp.zeros((R, 128), jnp.int32)
        row_r = lax.broadcasted_iota(jnp.int32, (128, 128), 0) & 7
        lane_full = lax.broadcasted_iota(jnp.int32, (1, 4, R, 128), 3)
        head4 = lax.broadcasted_iota(jnp.int32, (1, 4, R, 128), 1)
        first[2].wait()
        first[3].wait()
        table = jnp.zeros((R, 128), F32)
        ids_f = ids[...].astype(F32)
        route_f = route[...]
        for k in range(8):
            table = jnp.where(lane8 == k, ids_f[:, k : k + 1], table)
            table = jnp.where(lane8 == 8 + k, route_f[:, k : k + 1], table)
        recv_r[fx] = table
        first[1].wait()
        for r in range(R):
            filled = jnp.where(sub8 == r, lengths[r], filled)
        usable = ((cx * 128 + lane8) < filled)[None]
        first[0].wait()

        def attend(n, k):
            part = q_v[:, pl.ds(pl.multiple_of(k * 16 * HD, 16 * HD), 16 * HD)].astype(F32)
            queries = jnp.concatenate(
                [part[:, g * HD : (g + 1) * HD] for g in range(16)], axis=0
            ).astype(BF16)
            every = lax.dot_general(
                queries, k_v[n].reshape(R * 128, HD), (((1,), (1,)), ((), ())),
                preferred_element_type=F32,
            )
            scores = every[:, 0:128]
            for r in range(1, R):
                scores = jnp.where(row_r == r, every[:, r * 128 : (r + 1) * 128], scores)
            scores = (scores * HD ** (-0.5)).reshape(16, R, 128)
            peak = jnp.max(jnp.where(usable, scores, -1e30), axis=-1, keepdims=True)
            peak = peak.astype(BF16).astype(F32)
            probs = jnp.where(usable, jnp.exp(scores - peak), 0.0)
            probs = probs.astype(BF16).astype(F32)
            total = jnp.sum(probs, axis=-1, keepdims=True)
            flat = probs.reshape(128, 128)
            spread = jnp.concatenate(
                [jnp.where(row_r == r, flat, 0.0).astype(BF16) for r in range(R)], axis=1
            )
            numerator = jnp.dot(spread, v_v[n].reshape(R * 128, HD), preferred_element_type=F32)
            send_a[pl.ds(k * 4, 4), 0:4] = numerator.reshape(4, 4, R, HD).astype(BF16)
            peak4 = jnp.broadcast_to(peak, (16, R, 128)).reshape(4, 4, R, 128)
            total4 = jnp.broadcast_to(total, (16, R, 128)).reshape(4, 4, R, 128)
            high = total4.astype(BF16).astype(F32)
            marks = jnp.sum(
                jnp.where(lane_full == head4, peak4, 0.0)
                + jnp.where(lane_full == head4 + 4, high, 0.0)
                + jnp.where(lane_full == head4 + 8, total4 - high, 0.0),
                axis=1,
            )
            send_a[pl.ds(k * 4, 4), 4] = marks.astype(BF16)

    with jax.named_scope("attention"):
        for pair in kv_copies:
            for copy in pair:
                copy.wait()
        for n, step in enumerate(BLOCKS):
            attend(n, turn_x[step])

    with jax.named_scope("attention_sends"):
        pl.semaphore_wait(barrier, CTX - 1 + FFN - 1)
        for step in BLOCKS:
            for z in OTHERS + ((0,) if step else ()):
                to = turn_x[step] * SIDE + turn_z[z]
                push(send_a.at[to], recv_a.at[cx], 0, number_x[step] + number_z[z])
        every_ffn(lambda to: push(recv_r.at[fx], recv_r.at[fx], 1, to))
        recv_a[cx] = send_a[cx]
        lax.fori_loop(0, PER, fetch, 0)
        lax.fori_loop(0, E_LOC, fetch_down, 0)

    with jax.named_scope("routing"):
        settle(recv_r.at[pl.ds(0, FFN - 1)], recv_sem.at[1])
        tables = recv_r[...].reshape(FFN * R, 128)
        lane = lax.broadcasted_iota(jnp.int32, (FFN * R, 128), 1)
        token = lax.broadcasted_iota(jnp.int32, (FFN * R, 128), 0)
        expert = (fx * E_LOC + (lane >> 4)).astype(F32)
        chosen = jnp.zeros((FFN * R, 128), F32)
        weight = jnp.zeros((FFN * R, 128), F32)
        for k in range(8):
            hit = tables[:, k : k + 1] == expert
            chosen = jnp.where(hit, 1.0, chosen)
            weight = jnp.where(hit, tables[:, 8 + k : 9 + k], weight)
        row = lax.broadcasted_iota(jnp.int32, (64, 64), 0)
        col = lax.broadcasted_iota(jnp.int32, (64, 64), 1)
        before = jnp.where((col < row) & ((col >> 3) == (row >> 3)), 1.0, 0.0).astype(BF16)
        rank = jnp.dot(before, chosen.astype(BF16), preferred_element_type=F32)
        here = (
            (chosen > 0.5)
            & (rank == (lane & 1).astype(F32))
            & ((token >> 3) == ((lane & 15) >> 1))
        )
        here_f = jnp.where(here, 1.0, 0.0)
        padded = jnp.concatenate([here_f, jnp.zeros((64, 128), F32)], axis=0)
        pick[...] = jnp.transpose(padded).astype(BF16)
        weight = jnp.where(here, weight, 0.0)
        high = weight.astype(BF16)
        weigh[0:64] = high
        weigh[64:128] = (weight - high.astype(F32)).astype(BF16)

    with jax.named_scope("attention_wait"):
        settle(recv_a.at[pl.ds(0, CTX - 1)], recv_sem.at[0])

    with jax.named_scope("attention_combine"):
        got = recv_a[...].astype(F32)
        marks = got[:, 4]
        factor = jnp.exp(marks - jnp.max(marks, axis=0, keepdims=True))
        share = pltpu.roll(marks, 124, 2) + pltpu.roll(marks, 120, 2)
        below = jnp.sum(factor * share, axis=0)
        heads = []
        for h in range(4):
            top = jnp.zeros((R, HD), F32)
            for c in range(CTX):
                top = top + factor[c, :, h : h + 1] * got[c, h]
            heads.append(top / below[:, h : h + 1])
        attended = jnp.concatenate(heads, axis=1).astype(BF16)

        for copy in o_copies:
            copy.wait()

    with jax.named_scope("projection"):
        for half in HALVES:
            for step in half:
                block = turn_x[step]
                span = pl.ds(pl.multiple_of(block * 1024, 1024), 1024)
                projected = jnp.dot(attended, o_v[:, span], preferred_element_type=F32)
                for z in range(SIDE):
                    left, right = projected[:, z * 256 : z * 256 + 128], projected[:, z * 256 + 128 : z * 256 + 256]
                    send_b[block * SIDE + z] = jnp.concatenate([left, right], axis=0).astype(BF16)
            for step in half:
                for z in OTHERS + ((0,) if step else ()):
                    to = turn_x[step] * SIDE + turn_z[z]
                    push(send_b.at[to], recv_b.at[cx], 2, number_x[step] + number_z[z])
        recv_b[cx] = send_b[cx]

        def weights_here(e, carry):
            pltpu.make_async_copy(g_hbm.at[e], gu_v.at[e, :, 0:FFH], w_sem.at[0, e]).wait()
            pltpu.make_async_copy(u_hbm.at[e], gu_v.at[e, :, FFH:], w_sem.at[1, e]).wait()
            return carry

        first[4].wait()
        first[5].wait()
        res = residual[...].astype(F32)
        res = jnp.concatenate([res[:, 0:128], res[:, 128:256]], axis=0)

    with jax.named_scope("projection_wait"):
        settle(recv_b.at[pl.ds(0, CTX - 1)], recv_sem.at[2])

    with jax.named_scope("hidden_sends"):
        hidden = res + jnp.sum(recv_b[...].astype(F32), axis=0)
        recv_c[fx] = hidden.astype(BF16)
        every_ffn(lambda to: push(recv_c.at[fx], recv_c.at[fx], 3, to))
        lax.fori_loop(0, E_LOC, weights_here, 0)

    with jax.named_scope("hidden_wait"):
        settle(recv_c.at[pl.ds(0, FFN - 1)], recv_sem.at[3])

    with jax.named_scope("rows"):
        tokens = recv_c[...].astype(F32)
        left = tokens[:, 0:8, :].reshape(64, 128)
        right = tokens[:, 8:16, :].reshape(64, 128)
        gained = jnp.concatenate([left * gain[:, 0:128], right * gain[:, 128:256]], axis=1)
        gained = jnp.concatenate([gained, jnp.zeros((64, 256), F32)], axis=0).astype(BF16)
        rows[...] = (
            jnp.dot(pick[...], gained, preferred_element_type=F32)
            .astype(BF16)
            .reshape(E_LOC, SLOTS, COLS)
        )

        def share_squares():
            squares = jnp.sum(left * left + right * right, axis=1, keepdims=True).reshape(FFN, R, 1)
            squares = jnp.broadcast_to(squares, (FFN, R, 128))
            block = lax.broadcasted_iota(jnp.int32, (FFN, R, 128), 0)
            lanes = lax.broadcasted_iota(jnp.int32, (FFN, R, 128), 2)
            recv_s[0, sx] = jnp.sum(jnp.where(lanes == block, squares, 0.0), axis=0)
            for step in OTHERS:
                push(recv_s.at[0, sx], recv_s.at[0, sx], 6, first_line(0, step))

        def gate_up(g, step):
            e = g * PER + turn(g, step)
            both = jnp.dot(rows[e], gu_v[e], preferred_element_type=F32)
            return both[:, 0:FFH], both[:, FFH:]

    with jax.named_scope("gate_up"):
        for g in range(GROUPS):
            gate, upward = gate_up(g, 2)
            send_1[g, 4] = gate.astype(BF16)
            send_1[g, 5] = upward.astype(BF16)
        for g in range(GROUPS):
            push(send_1.at[g, 5], passing.at[g], 9 + g, first_line(g, 3))
            push(send_1.at[g, 4], recv_1.at[g, 4], 4 + g, first_line(g, 2))
        share_squares()
        for g in range(GROUPS):
            gate, upward = gate_up(g, 1)
            send_1[g, 0] = gate.astype(BF16)
            send_1[g, 1] = upward.astype(BF16)
        for g in range(GROUPS):
            push(send_1.at[g, pl.ds(0, 2)], recv_1.at[g, pl.ds(0, 2)], 4 + g, first_line(g, 1))
        for g in range(GROUPS):
            gate, behind[g] = gate_up(g, 3)
            send_1[g, 2] = gate.astype(BF16)
        for g in range(GROUPS):
            push(send_1.at[g, 2], recv_1.at[g, 2], 4 + g, first_line(g, 3))
        for g in range(GROUPS):
            own_1[g, 0], own_1[g, 1] = gate_up(g, 0)
        for g in range(GROUPS):
            settle(passing.at[g], recv_sem.at[9 + g])
            send_1[g, 3] = (behind[g] + passing[g].astype(F32)).astype(BF16)
            push(send_1.at[g, 3], recv_1.at[g, 3], 4 + g, first_line(g, 3))

    with jax.named_scope("square_sums"):
        settle(recv_s.at[0, pl.ds(0, SIDE - 1)], recv_sem.at[6])
        recv_s[1, sz] = jnp.sum(recv_s[0], axis=0)
        for step in OTHERS:
            push(recv_s.at[1, sz], recv_s.at[1, sz], 12, second_line(0, step))

    with jax.named_scope("first_sums"):
        for g in range(GROUPS):
            after = place(g)[1]
            settle(recv_1.at[g], recv_sem.at[4 + g])
            gate = own_1[g, 0]
            upward = own_1[g, 1]
            for c in (0, 2, 4):
                gate = gate + recv_1[g, c].astype(F32)
            for c in (1, 3):
                upward = upward + recv_1[g, c].astype(F32)
            for n in range(SIDE):
                span = slice(n * QUARTER, (n + 1) * QUARTER)
                send_2[g, n, 0:SLOTS] = gate[:, span].astype(BF16)
                send_2[g, n, SLOTS:] = upward[:, span].astype(BF16)
            for step in OTHERS:
                to = turn(1 - g, step)
                push(send_2.at[g, to], recv_2.at[g, after], 7 + g, second_line(g, step))
            recv_2[g, after] = send_2[g, after]

    with jax.named_scope("scales"):
        settle(recv_s.at[1, pl.ds(0, SIDE - 1)], recv_sem.at[12])
        scale = lax.rsqrt(jnp.sum(recv_s[1], axis=0) * (1.0 / D) + 1e-06)
        scale = jnp.concatenate(
            [jnp.broadcast_to(scale[:, b : b + 1], (R, 128)) for b in range(FFN)]
            + [jnp.zeros((64, 128), F32)],
            axis=0,
        )
        high = scale.astype(BF16)
        split = jnp.concatenate([high, (scale - high.astype(F32)).astype(BF16)], axis=1)
        owned = [
            pick[pl.ds(pl.multiple_of((g * PER + place(g)[0]) * SLOTS, SLOTS), SLOTS), :]
            for g in range(GROUPS)
        ]
        scales = jnp.dot(jnp.concatenate(owned, axis=0), split, preferred_element_type=F32)
        scales = scales[:, 0:128] + scales[:, 128:256]
        own_scales = [
            jnp.concatenate([scales[g * SLOTS : (g + 1) * SLOTS]] * (QUARTER // 128), axis=1)
            for g in range(GROUPS)
        ]

    with jax.named_scope("inner"):
        for g in range(GROUPS):
            settle(recv_2.at[g, pl.ds(0, SIDE - 1)], recv_sem.at[7 + g])
            both = recv_2[g, 0].astype(F32)
            for c in range(1, SIDE):
                both = both + recv_2[g, c].astype(F32)
            gate = both[0:SLOTS] * own_scales[g]
            upward = both[SLOTS:] * own_scales[g]
            inner = gate / (1.0 + jnp.exp(-gate)) * upward
            recv_e[sx, sz, g] = inner.astype(BF16)

    with jax.named_scope("inner_sends"):
        for dx, dz in FAR_FIRST:
            push(
                recv_e.at[sx, sz], recv_e.at[sx, sz], 13, number_x[dx] + number_z[dz], line_recv.at[sx]
            )

        def down_here(e, carry):
            pltpu.make_async_copy(d_hbm.at[e], d_v.at[e], w_sem.at[2, e]).wait()
            return carry

        lax.fori_loop(0, E_LOC, down_here, 0)

    with jax.named_scope("down"):
        for step in (0, 1, 3, 2):
            x = turn_x[step]
            settle(recv_e.at[0, pl.ds(0, SIDE if step else SIDE - 1)], line_recv.at[x])
            inner = jnp.concatenate([recv_e[x, q, 0] for q in range(SIDE)], axis=1)
            results[x] = jnp.dot(inner, d_v[x], preferred_element_type=F32).astype(BF16)
            span = pl.ds(pl.multiple_of(x * QUARTER, QUARTER), QUARTER)
            for n in range(PER):
                term = jnp.dot(recv_e[x, n, 1], d_v[PER + n, span, :], preferred_element_type=F32)
                if step:
                    term = term + partly[n]
                if step != 2:
                    partly[n] = term
                else:
                    results[PER + n] = term.astype(BF16)

    with jax.named_scope("mix"):
        found = results[...].reshape(E_LOC * SLOTS, COLS)
        mixed = jnp.dot(weigh[...], found, preferred_element_type=F32)
        mixed = mixed[0:64] + mixed[64:128]
        for b in range(FFN):
            piece = mixed[b * R : (b + 1) * R]
            send_f[b] = piece.astype(BF16)
        for step in FFN_FIRST:
            push(send_f.at[lax.rem(fx + step, FFN)], out.at[fx], 11, number_f[step])
        kept = pltpu.make_async_copy(send_f.at[fx], out.at[fx], o_sem.at[0])
        kept.start()

    with jax.named_scope("last_wait"):
        settle(send_a.at[pl.ds(0, CTX - 1)], send_sem.at[0])
        settle(recv_r.at[pl.ds(0, FFN - 1)], send_sem.at[1])
        settle(send_b.at[pl.ds(0, CTX - 1)], send_sem.at[2])
        settle(recv_c.at[pl.ds(0, FFN - 1)], send_sem.at[3])
        settle(recv_s.at[0, pl.ds(0, SIDE - 1)], send_sem.at[6])
        settle(recv_s.at[1, pl.ds(0, SIDE - 1)], send_sem.at[12])
        for g in range(GROUPS):
            settle(recv_1.at[g], send_sem.at[4 + g])
            settle(passing.at[g], send_sem.at[9 + g])
            settle(send_2.at[g, pl.ds(0, SIDE - 1)], send_sem.at[7 + g])
        settle(recv_e.at[pl.ds(0, SIDE - 1)], send_sem.at[13])
        settle(recv_e.at[0, pl.ds(0, SIDE - 1)], send_sem.at[13])
        settle(send_f.at[pl.ds(0, FFN - 1)], send_sem.at[11])

        kept.wait()
        settle(out.at[pl.ds(0, FFN - 1)], recv_sem.at[11])


def local(
    queries, key_cache, value_cache, lengths, residual, o_weight, norm_gain,
    gate_proj, up_proj, down_proj, expert_ids, route_weight,
):
    anywhere = pl.BlockSpec(memory_space=pl.ANY)
    parts = pl.pallas_call(
        kernel,
        out_shape=pltpu.VMEM((FFN, R, COLS), BF16),
        in_specs=[anywhere] * 12,
        out_specs=pl.BlockSpec(memory_space=pltpu.VMEM),
        scratch_shapes=[
            pltpu.SMEM((R,), jnp.int32),
            pltpu.VMEM((R, COLS), BF16),
            pltpu.VMEM((1, COLS), F32),
            pltpu.VMEM((R, 8), jnp.int32),
            pltpu.VMEM((R, 8), F32),
            pltpu.VMEM((R, HQ * HD), BF16),
            pltpu.VMEM((KVH, R, 128, HD), BF16),
            pltpu.VMEM((KVH, R, 128, HD), BF16),
            pltpu.VMEM((HQ * HD // CTX, D), BF16),
            pltpu.VMEM((E_LOC, COLS, 2 * FFH), BF16),
            pltpu.VMEM((E_LOC, FFH, COLS), BF16),
            pltpu.VMEM((CTX, 5, R, 128), BF16),
            pltpu.VMEM((CTX, 5, R, 128), BF16),
            pltpu.VMEM((CTX, 16, 128), BF16),
            pltpu.VMEM((CTX, 16, 128), BF16),
            pltpu.VMEM((FFN, 16, 128), BF16),
            pltpu.VMEM((FFN, R, 128), F32),
            pltpu.VMEM((2, SIDE, R, 128), F32),
            pltpu.VMEM((GROUPS, 6, SLOTS, FFH), BF16),
            pltpu.VMEM((GROUPS, SLOTS, FFH), BF16),
            pltpu.VMEM((GROUPS, SLOTS, FFH), F32),
            pltpu.VMEM((GROUPS, 2, SLOTS, FFH), F32),
            pltpu.VMEM((GROUPS, 5, SLOTS, FFH), BF16),
            pltpu.VMEM((GROUPS, SIDE, 2 * SLOTS, QUARTER), BF16),
            pltpu.VMEM((GROUPS, SIDE, 2 * SLOTS, QUARTER), BF16),
            pltpu.VMEM((SIDE, SIDE, GROUPS, SLOTS, QUARTER), BF16),
            pltpu.VMEM((FFN, R, COLS), BF16),
            pltpu.VMEM((128, 128), BF16),
            pltpu.VMEM((128, 128), BF16),
            pltpu.VMEM((E_LOC, SLOTS, COLS), BF16),
            pltpu.VMEM((E_LOC, SLOTS, COLS), BF16),
            pltpu.VMEM((PER, SLOTS, COLS), F32),
            pltpu.SemaphoreType.DMA((6,)),
            pltpu.SemaphoreType.DMA((2, KVH)),
            pltpu.SemaphoreType.DMA((4,)),
            pltpu.SemaphoreType.DMA((3, E_LOC)),
            pltpu.SemaphoreType.DMA((14,)),
            pltpu.SemaphoreType.DMA((14,)),
            pltpu.SemaphoreType.DMA((SIDE,)),
        ],
        compiler_params=pltpu.CompilerParams(
            collective_id=0, has_side_effects=True, vmem_limit_bytes=56 * 2**20
        ),
        cost_estimate=pl.CostEstimate(
            flops=1_000_000_000, bytes_accessed=26_000_000, transcendentals=100_000
        ),
    )(
        lengths, residual, norm_gain.reshape(1, COLS), expert_ids, route_weight,
        queries, key_cache, value_cache, o_weight, gate_proj, up_proj, down_proj,
    )
    return jnp.sum(parts.astype(F32), axis=0).astype(BF16)


def solution(mesh):
    placed = (
        P("ffn", None),
        P("ffn", "ctx", None),
        P("ffn", "ctx", None),
        P("ffn"),
        P("ffn", "ctx"),
        P("ctx", None),
        P("ctx"),
        P("ffn", "ctx", None),
        P("ffn", "ctx", None),
        P("ffn", None, "ctx"),
        P("ffn", None),
        P("ffn", None),
    )
    return jax.shard_map(
        local, mesh=mesh, in_specs=placed, out_specs=P("ffn", "ctx"), check_vma=False
    )
```

time: 403 us -> 46.1 us (0.11)
  waiting for transfers between devices: 214 us -> 0 us
  blocking collectives: 152 us -> 0 us
  Pallas kernels: 0 us -> 45.4 us
  matrix products: 18.9 us -> 0 us
  between operations: 13.2 us -> 0.01 us
    psum x2 -> x0, waiting for transfers between devices: 143 us -> none  [the longest x1 79.7 us: local(): lax.psum(up_part.astype(jnp.bfloat16), 'ctx').astype(jnp.float32)]
    reduce_scatter x1 -> x0, waiting for transfers between devices: 70.6 us -> none  [local(): lax.psum_scatter(projected, 'ctx', scatter_dimension=1, tiled=True)]
    pmax x1 -> x0, blocking collectives: 62.4 us -> none  [local(): peak_score = lax.pmax(jnp.max(masked, axis=-1, keepdims=True), 'ctx')]
    psum x2 -> x0, blocking collectives: 59.4 us -> none  [the longest x1 30.9 us: local(): lax.psum(jnp.sum(hidden_f * hidden_f, axis=-1, keepdims=True), 'ctx')]
    pallas_call x0 -> x1, Pallas kernels: none -> 45.4 us  [local(): pl.pallas_call(kernel, out_shape=pltpu.VMEM((FFN, R, COLS), BF16), in_spe...]
    all_to_all x2 -> x0, blocking collectives: 29.7 us -> none  [the longest x1 18.7 us: local(): lax.all_to_all(outgoing, 'ffn', split_axis=1, concat_axis=1, tiled=True)]
    dot_general x8 -> x0, matrix products: 18.9 us -> none  [the longest x1 4.62 us: local(): jnp.einsum('esd,edf->esf', expert_rows, up_proj, preferred_element_type=j...]
  transfers between devices with their start and end apart: 3 -> 0, of which waited for: 3 -> 0; matrix products, arithmetic and copies ran while one was open for 0% -> 0% of each run, Pallas kernels for 0% -> 0%
where the time goes in v2:
time: 46.1 us; the launch traced here: 46 us
  Pallas kernels  45.4 us (98%)
  other arithmetic  0.61 us (1%)
    pallas_call x1, Pallas kernels, local(): pl.pallas_call(kernel, out_shape=pltpu.VMEM((FFN, R, COLS), BF16), in_spe...  45.4 us

profile of v2, /device:TPU:1, one launch (start us, length us, event | category | flops | bytes accessed | tf_op | source)
XLA Modules:
  0.0 46.0 jit_solution(16695051412156671836)
XLA Ops:
  0.0 45.4 %shard_map.118 = bf16[8,8,256]{2,1,0:T(8,128)(2,1)S(1)} custom-call(s32[8]{0:T(128)} %len_hbm.1, bf16[8,256]{1,0:T(8,128)(2,1)} %res_hbm.1, f32[1,256]{1,0:T(1,128)} %bitcast.1, s32[8,8]{1,0:T(8,128)} %ids_hbm.1, f32[8,8]{1,0:T(8,128)} %route_hbm.1, bf16[8,8192]{1,0:T(8,128)(2,1)} %q_hbm.1, bf16[8,128,512]{2,1,0:T(8,128)(2,1)} %k_hbm.1, ...), custom_call_target="tpu_custom_call" | custom-call | flops 1000000000 | bytes 26000000 | tf_op jit(solution)/shard_map/pallas_call | solution.py:473
  45.4 0.6 %reduce_sum.12 = bf16[8,256]{1,0:T(8,128)(2,1)} reduce(bf16[8,8,256]{2,1,0:T(8,128)(2,1)S(1)} %shard_map.118, bf16[]{:T(256)} %constant.2.clone.1), dimensions={0}, to_apply=%region_0.0 | reduce | flops 14336 | bytes 36866 | tf_op jit(solution)/shard_map/reduce_sum | solution.py:529

commit v3 on v2

--- a/solution.py
+++ b/solution.py
@@ -33,7 +33,6 @@
 FFN_FIRST = (4, 5, 3, 2, 6, 7, 1)
 OTHERS = (2, 1, 3)
 BLOCKS = (2, 1, 3, 0)
-HALVES = ((2, 1), (3, 0))
 
 
 def kernel(
@@ -98,17 +97,14 @@
         for copy in first[:4]:
             copy.start()
         kv_copies = []
-        for n, step in enumerate(BLOCKS):
-            k = turn_x[step]
-            span = pl.ds(pl.multiple_of(k * HD, HD), HD)
-            kv_copies.append(
-                (
-                    pltpu.make_async_copy(k_hbm.at[:, :, span], k_v.at[n], kv_sem.at[0, n]),
-                    pltpu.make_async_copy(v_hbm.at[:, :, span], v_v.at[n], kv_sem.at[1, n]),
+        for n in range(2):
+            for m, (src, dst) in enumerate(((k_hbm, k_v), (v_hbm, v_v))):
+                span = pl.ds(n * (R // 2), R // 2)
+                kv_copies.append(
+                    pltpu.make_async_copy(src.at[span], dst.at[span], kv_sem.at[m, n])
                 )
-            )
-            for copy in kv_copies[n]:
-                copy.start()
+        for copy in kv_copies:
+            copy.start()
         for copy in first[4:]:
             copy.start()
         for dx, dz in FAR_FIRST:
@@ -157,14 +153,14 @@
         usable = ((cx * 128 + lane8) < filled)[None]
         first[0].wait()
 
-        def attend(n, k):
-            part = q_v[:, pl.ds(pl.multiple_of(k * 16 * HD, 16 * HD), 16 * HD)].astype(F32)
+        def attend(k):
+            part = q_v[:, k * 16 * HD : (k + 1) * 16 * HD].astype(F32)
             queries = jnp.concatenate(
                 [part[:, g * HD : (g + 1) * HD] for g in range(16)], axis=0
             ).astype(BF16)
             every = lax.dot_general(
-                queries, k_v[n].reshape(R * 128, HD), (((1,), (1,)), ((), ())),
-                preferred_element_type=F32,
+                queries, k_v[:, :, k * HD : (k + 1) * HD].reshape(R * 128, HD),
+                (((1,), (1,)), ((), ())), preferred_element_type=F32,
             )
             scores = every[:, 0:128]
             for r in range(1, R):
@@ -179,8 +175,9 @@
             spread = jnp.concatenate(
                 [jnp.where(row_r == r, flat, 0.0).astype(BF16) for r in range(R)], axis=1
             )
-            numerator = jnp.dot(spread, v_v[n].reshape(R * 128, HD), preferred_element_type=F32)
-            send_a[pl.ds(k * 4, 4), 0:4] = numerator.reshape(4, 4, R, HD).astype(BF16)
+            values = v_v[:, :, k * HD : (k + 1) * HD].reshape(R * 128, HD)
+            numerator = jnp.dot(spread, values, preferred_element_type=F32)
+            send_a[k * 4 : (k + 1) * 4, 0:4] = numerator.reshape(4, 4, R, HD).astype(BF16)
             peak4 = jnp.broadcast_to(peak, (16, R, 128)).reshape(4, 4, R, 128)
             total4 = jnp.broadcast_to(total, (16, R, 128)).reshape(4, 4, R, 128)
             high = total4.astype(BF16).astype(F32)
@@ -190,14 +187,13 @@
                 + jnp.where(lane_full == head4 + 8, total4 - high, 0.0),
                 axis=1,
             )
-            send_a[pl.ds(k * 4, 4), 4] = marks.astype(BF16)
+            send_a[k * 4 : (k + 1) * 4, 4] = marks.astype(BF16)
 
     with jax.named_scope("attention"):
-        for pair in kv_copies:
-            for copy in pair:
-                copy.wait()
-        for n, step in enumerate(BLOCKS):
-            attend(n, turn_x[step])
+        for copy in kv_copies:
+            copy.wait()
+        for k in range(KVH):
+            attend(k)
 
     with jax.named_scope("attention_sends"):
         pl.semaphore_wait(barrier, CTX - 1 + FFN - 1)
@@ -260,18 +256,14 @@
             copy.wait()
 
     with jax.named_scope("projection"):
-        for half in HALVES:
-            for step in half:
-                block = turn_x[step]
-                span = pl.ds(pl.multiple_of(block * 1024, 1024), 1024)
-                projected = jnp.dot(attended, o_v[:, span], preferred_element_type=F32)
-                for z in range(SIDE):
-                    left, right = projected[:, z * 256 : z * 256 + 128], projected[:, z * 256 + 128 : z * 256 + 256]
-                    send_b[block * SIDE + z] = jnp.concatenate([left, right], axis=0).astype(BF16)
-            for step in half:
-                for z in OTHERS + ((0,) if step else ()):
-                    to = turn_x[step] * SIDE + turn_z[z]
-                    push(send_b.at[to], recv_b.at[cx], 2, number_x[step] + number_z[z])
+        projected = jnp.dot(attended, o_v[...], preferred_element_type=F32)
+        for c in range(CTX):
+            ahead, rest = projected[:, c * 256 : c * 256 + 128], projected[:, c * 256 + 128 : c * 256 + 256]
+            send_b[c] = jnp.concatenate([ahead, rest], axis=0).astype(BF16)
+        for step in BLOCKS:
+            for z in OTHERS + ((0,) if step else ()):
+                to = turn_x[step] * SIDE + turn_z[z]
+                push(send_b.at[to], recv_b.at[cx], 2, number_x[step] + number_z[z])
         recv_b[cx] = send_b[cx]
 
         def weights_here(e, carry):
@@ -330,20 +322,18 @@
         for g in range(GROUPS):
             push(send_1.at[g, 5], passing.at[g], 9 + g, first_line(g, 3))
             push(send_1.at[g, 4], recv_1.at[g, 4], 4 + g, first_line(g, 2))
-        share_squares()
         for g in range(GROUPS):
             gate, upward = gate_up(g, 1)
             send_1[g, 0] = gate.astype(BF16)
             send_1[g, 1] = upward.astype(BF16)
-        for g in range(GROUPS):
-            push(send_1.at[g, pl.ds(0, 2)], recv_1.at[g, pl.ds(0, 2)], 4 + g, first_line(g, 1))
-        for g in range(GROUPS):
             gate, behind[g] = gate_up(g, 3)
             send_1[g, 2] = gate.astype(BF16)
         for g in range(GROUPS):
+            push(send_1.at[g, pl.ds(0, 2)], recv_1.at[g, pl.ds(0, 2)], 4 + g, first_line(g, 1))
             push(send_1.at[g, 2], recv_1.at[g, 2], 4 + g, first_line(g, 3))
         for g in range(GROUPS):
             own_1[g, 0], own_1[g, 1] = gate_up(g, 0)
+        share_squares()
         for g in range(GROUPS):
             settle(passing.at[g], recv_sem.at[9 + g])
             send_1[g, 3] = (behind[g] + passing[g].astype(F32)).astype(BF16)
@@ -482,8 +472,8 @@
             pltpu.VMEM((R, 8), jnp.int32),
             pltpu.VMEM((R, 8), F32),
             pltpu.VMEM((R, HQ * HD), BF16),
-            pltpu.VMEM((KVH, R, 128, HD), BF16),
-            pltpu.VMEM((KVH, R, 128, HD), BF16),
+            pltpu.VMEM((R, 128, KVH * HD), BF16),
+            pltpu.VMEM((R, 128, KVH * HD), BF16),
             pltpu.VMEM((HQ * HD // CTX, D), BF16),
             pltpu.VMEM((E_LOC, COLS, 2 * FFH), BF16),
             pltpu.VMEM((E_LOC, FFH, COLS), BF16),
@@ -509,7 +499,7 @@
             pltpu.VMEM((E_LOC, SLOTS, COLS), BF16),
             pltpu.VMEM((PER, SLOTS, COLS), F32),
             pltpu.SemaphoreType.DMA((6,)),
-            pltpu.SemaphoreType.DMA((2, KVH)),
+            pltpu.SemaphoreType.DMA((2, 2)),
             pltpu.SemaphoreType.DMA((4,)),
             pltpu.SemaphoreType.DMA((3, E_LOC)),
             pltpu.SemaphoreType.DMA((14,)),

time: 46.1 us -> 46.1 us (level)
  no operation moved by 1% of the time
where the time goes in v3:
time: 46.1 us; the launch traced here: 46 us
  Pallas kernels  45.4 us (98%)
  other arithmetic  0.61 us (1%)
    pallas_call x1, Pallas kernels, local(): pl.pallas_call(kernel, out_shape=pltpu.VMEM((FFN, R, COLS), BF16), in_spe...  45.4 us

profile of v3, /device:TPU:1, one launch (start us, length us, event | category | flops | bytes accessed | tf_op | source)
XLA Modules:
  0.0 46.0 jit_solution(204881542024986586)
XLA Ops:
  0.0 45.4 %shard_map.118 = bf16[8,8,256]{2,1,0:T(8,128)(2,1)S(1)} custom-call(s32[8]{0:T(128)} %len_hbm.1, bf16[8,256]{1,0:T(8,128)(2,1)} %res_hbm.1, f32[1,256]{1,0:T(1,128)} %bitcast.1, s32[8,8]{1,0:T(8,128)} %ids_hbm.1, f32[8,8]{1,0:T(8,128)} %route_hbm.1, bf16[8,8192]{1,0:T(8,128)(2,1)} %q_hbm.1, bf16[8,128,512]{2,1,0:T(8,128)(2,1)} %k_hbm.1, ...), custom_call_target="tpu_custom_call" | custom-call | flops 1000000000 | bytes 26000000 | tf_op jit(solution)/shard_map/pallas_call | solution.py:463
  45.4 0.6 %reduce_sum.12 = bf16[8,256]{1,0:T(8,128)(2,1)} reduce(bf16[8,8,256]{2,1,0:T(8,128)(2,1)S(1)} %shard_map.118, bf16[]{:T(256)} %constant.2.clone.1), dimensions={0}, to_apply=%region_0.0 | reduce | flops 14336 | bytes 36866 | tf_op jit(solution)/shard_map/reduce_sum | solution.py:519

commit v4 on v3

--- a/solution.py
+++ b/solution.py
@@ -51,8 +51,9 @@
     sx = cx // SIDE
     sz = lax.rem(cx, SIDE)
 
-    turn_x = [lax.rem(sx + step, SIDE) for step in range(SIDE)]
-    turn_z = [lax.rem(sz + step, SIDE) for step in range(SIDE)]
+    way = 1 - 2 * lax.rem(fx, 2)
+    turn_x = [lax.rem(sx + SIDE + way * step, SIDE) for step in range(SIDE)]
+    turn_z = [lax.rem(sz + SIDE + way * step, SIDE) for step in range(SIDE)]
     number_x = [x * (SIDE * FFN) for x in turn_x]
     number_z = [z * FFN + fx for z in turn_z]
     number_f = [cx * FFN + lax.rem(fx + step, FFN) for step in range(FFN)]
@@ -97,8 +98,8 @@
         for copy in first[:4]:
             copy.start()
         kv_copies = []
-        for n in range(2):
-            for m, (src, dst) in enumerate(((k_hbm, k_v), (v_hbm, v_v))):
+        for m, (src, dst) in enumerate(((k_hbm, k_v), (v_hbm, v_v))):
+            for n in range(2):
                 span = pl.ds(n * (R // 2), R // 2)
                 kv_copies.append(
                     pltpu.make_async_copy(src.at[span], dst.at[span], kv_sem.at[m, n])
@@ -117,15 +118,12 @@
             for n in range(4)
         ]
 
-        for copy in o_copies:
-            copy.start()
-
-        def fetch(n, carry):
+
+        def fetch(step):
             for g in range(GROUPS):
-                e = g * PER + lax.rem(place(g)[0] + SIDE - 1 - n, SIDE)
+                e = g * PER + turn(g, step)
                 pltpu.make_async_copy(g_hbm.at[e], gu_v.at[e, :, 0:FFH], w_sem.at[0, e]).start()
                 pltpu.make_async_copy(u_hbm.at[e], gu_v.at[e, :, FFH:], w_sem.at[1, e]).start()
-            return carry
 
         def fetch_down(e, carry):
             pltpu.make_async_copy(d_hbm.at[e], d_v.at[e], w_sem.at[2, e]).start()
@@ -153,7 +151,7 @@
         usable = ((cx * 128 + lane8) < filled)[None]
         first[0].wait()
 
-        def attend(k):
+        def weigh_up(k):
             part = q_v[:, k * 16 * HD : (k + 1) * 16 * HD].astype(F32)
             queries = jnp.concatenate(
                 [part[:, g * HD : (g + 1) * HD] for g in range(16)], axis=0
@@ -171,13 +169,6 @@
             probs = jnp.where(usable, jnp.exp(scores - peak), 0.0)
             probs = probs.astype(BF16).astype(F32)
             total = jnp.sum(probs, axis=-1, keepdims=True)
-            flat = probs.reshape(128, 128)
-            spread = jnp.concatenate(
-                [jnp.where(row_r == r, flat, 0.0).astype(BF16) for r in range(R)], axis=1
-            )
-            values = v_v[:, :, k * HD : (k + 1) * HD].reshape(R * 128, HD)
-            numerator = jnp.dot(spread, values, preferred_element_type=F32)
-            send_a[k * 4 : (k + 1) * 4, 0:4] = numerator.reshape(4, 4, R, HD).astype(BF16)
             peak4 = jnp.broadcast_to(peak, (16, R, 128)).reshape(4, 4, R, 128)
             total4 = jnp.broadcast_to(total, (16, R, 128)).reshape(4, 4, R, 128)
             high = total4.astype(BF16).astype(F32)
@@ -188,12 +179,26 @@
                 axis=1,
             )
             send_a[k * 4 : (k + 1) * 4, 4] = marks.astype(BF16)
+            return probs.reshape(128, 128)
+
+        def sum_up(k, flat):
+            spread = jnp.concatenate(
+                [jnp.where(row_r == r, flat, 0.0).astype(BF16) for r in range(R)], axis=1
+            )
+            values = v_v[:, :, k * HD : (k + 1) * HD].reshape(R * 128, HD)
+            numerator = jnp.dot(spread, values, preferred_element_type=F32)
+            send_a[k * 4 : (k + 1) * 4, 0:4] = numerator.reshape(4, 4, R, HD).astype(BF16)
 
     with jax.named_scope("attention"):
-        for copy in kv_copies:
-            copy.wait()
+        kv_copies[0].wait()
+        kv_copies[1].wait()
+        flats = [weigh_up(k) for k in range(KVH)]
+        kv_copies[2].wait()
+        kv_copies[3].wait()
+        for copy in o_copies:
+            copy.start()
         for k in range(KVH):
-            attend(k)
+            sum_up(k, flats[k])
 
     with jax.named_scope("attention_sends"):
         pl.semaphore_wait(barrier, CTX - 1 + FFN - 1)
@@ -203,8 +208,8 @@
                 push(send_a.at[to], recv_a.at[cx], 0, number_x[step] + number_z[z])
         every_ffn(lambda to: push(recv_r.at[fx], recv_r.at[fx], 1, to))
         recv_a[cx] = send_a[cx]
-        lax.fori_loop(0, PER, fetch, 0)
-        lax.fori_loop(0, E_LOC, fetch_down, 0)
+        fetch(2)
+        fetch(1)
 
     with jax.named_scope("routing"):
         settle(recv_r.at[pl.ds(0, FFN - 1)], recv_sem.at[1])
@@ -265,6 +270,8 @@
                 to = turn_x[step] * SIDE + turn_z[z]
                 push(send_b.at[to], recv_b.at[cx], 2, number_x[step] + number_z[z])
         recv_b[cx] = send_b[cx]
+        fetch(3)
+        fetch(0)
 
         def weights_here(e, carry):
             pltpu.make_async_copy(g_hbm.at[e], gu_v.at[e, :, 0:FFH], w_sem.at[0, e]).wait()
@@ -283,6 +290,7 @@
         hidden = res + jnp.sum(recv_b[...].astype(F32), axis=0)
         recv_c[fx] = hidden.astype(BF16)
         every_ffn(lambda to: push(recv_c.at[fx], recv_c.at[fx], 3, to))
+        lax.fori_loop(0, E_LOC, fetch_down, 0)
         lax.fori_loop(0, E_LOC, weights_here, 0)
 
     with jax.named_scope("hidden_wait"):

time: 46.1 us -> 46 us (level)
  no operation moved by 1% of the time
where the time goes in v4:
time: 46 us; the launch traced here: 45.8 us
  Pallas kernels  45.2 us (98%)
  other arithmetic  0.61 us (1%)
    pallas_call x1, Pallas kernels, local(): pl.pallas_call(kernel, out_shape=pltpu.VMEM((FFN, R, COLS), BF16), in_spe...  45.2 us

profile of v4, /device:TPU:1, one launch (start us, length us, event | category | flops | bytes accessed | tf_op | source)
XLA Modules:
  0.0 45.8 jit_solution(12605292032942078347)
XLA Ops:
  0.0 45.2 %shard_map.118 = bf16[8,8,256]{2,1,0:T(8,128)(2,1)S(1)} custom-call(s32[8]{0:T(128)} %len_hbm.1, bf16[8,256]{1,0:T(8,128)(2,1)} %res_hbm.1, f32[1,256]{1,0:T(1,128)} %bitcast.1, s32[8,8]{1,0:T(8,128)} %ids_hbm.1, f32[8,8]{1,0:T(8,128)} %route_hbm.1, bf16[8,8192]{1,0:T(8,128)(2,1)} %q_hbm.1, bf16[8,128,512]{2,1,0:T(8,128)(2,1)} %k_hbm.1, ...), custom_call_target="tpu_custom_call" | custom-call | flops 1000000000 | bytes 26000000 | tf_op jit(solution)/shard_map/pallas_call | solution.py:471
  45.2 0.6 %reduce_sum.12 = bf16[8,256]{1,0:T(8,128)(2,1)} reduce(bf16[8,8,256]{2,1,0:T(8,128)(2,1)S(1)} %shard_map.118, bf16[]{:T(256)} %constant.2.clone.1), dimensions={0}, to_apply=%region_0.0 | reduce | flops 14336 | bytes 36866 | tf_op jit(solution)/shard_map/reduce_sum | solution.py:527

commit v5 on v4

--- a/solution.py
+++ b/solution.py
@@ -42,7 +42,7 @@
     lengths, residual, gain, ids, route,
     q_v, k_v, v_v, o_v, gu_v, d_v,
     send_a, recv_a, send_b, recv_b, recv_c, recv_r, recv_s,
-    send_1, passing, behind, own_1, recv_1, send_2, recv_2, recv_e, send_f,
+    send_1, passing, behind, own_1, recv_1, send_2, recv_2, recv_e, send_f, recv_f,
     pick, weigh, rows, results, partly,
     in_sem, kv_sem, o_sem, w_sem, send_sem, recv_sem, line_recv,
 ):
@@ -56,6 +56,11 @@
     turn_z = [lax.rem(sz + SIDE + way * step, SIDE) for step in range(SIDE)]
     number_x = [x * (SIDE * FFN) for x in turn_x]
     number_z = [z * FFN + fx for z in turn_z]
+    odd = lax.rem(fx, 2)
+    outer_number = [x + odd * (z - x) for x, z in zip(number_x, number_z)]
+    inner_number = [z + odd * (x - z) for x, z in zip(number_x, number_z)]
+    outer_place = [x * SIDE + odd * (z - x * SIDE) for x, z in zip(turn_x, turn_z)]
+    inner_place = [z + odd * (x * SIDE - z) for x, z in zip(turn_x, turn_z)]
     number_f = [cx * FFN + lax.rem(fx + step, FFN) for step in range(FFN)]
 
     def every_ffn(visit):
@@ -204,8 +209,8 @@
         pl.semaphore_wait(barrier, CTX - 1 + FFN - 1)
         for step in BLOCKS:
             for z in OTHERS + ((0,) if step else ()):
-                to = turn_x[step] * SIDE + turn_z[z]
-                push(send_a.at[to], recv_a.at[cx], 0, number_x[step] + number_z[z])
+                to = outer_place[step] + inner_place[z]
+                push(send_a.at[to], recv_a.at[cx], 0, outer_number[step] + inner_number[z])
         every_ffn(lambda to: push(recv_r.at[fx], recv_r.at[fx], 1, to))
         recv_a[cx] = send_a[cx]
         fetch(2)
@@ -267,8 +272,8 @@
             send_b[c] = jnp.concatenate([ahead, rest], axis=0).astype(BF16)
         for step in BLOCKS:
             for z in OTHERS + ((0,) if step else ()):
-                to = turn_x[step] * SIDE + turn_z[z]
-                push(send_b.at[to], recv_b.at[cx], 2, number_x[step] + number_z[z])
+                to = outer_place[step] + inner_place[z]
+                push(send_b.at[to], recv_b.at[cx], 2, outer_number[step] + inner_number[z])
         recv_b[cx] = send_b[cx]
         fetch(3)
         fetch(0)
@@ -407,7 +412,8 @@
     with jax.named_scope("inner_sends"):
         for dx, dz in FAR_FIRST:
             push(
-                recv_e.at[sx, sz], recv_e.at[sx, sz], 13, number_x[dx] + number_z[dz], line_recv.at[sx]
+                recv_e.at[sx, sz], recv_e.at[sx, sz], 13, outer_number[dx] + inner_number[dz],
+                line_recv.at[sx],
             )
 
         def down_here(e, carry):
@@ -440,9 +446,8 @@
             piece = mixed[b * R : (b + 1) * R]
             send_f[b] = piece.astype(BF16)
         for step in FFN_FIRST:
-            push(send_f.at[lax.rem(fx + step, FFN)], out.at[fx], 11, number_f[step])
-        kept = pltpu.make_async_copy(send_f.at[fx], out.at[fx], o_sem.at[0])
-        kept.start()
+            push(send_f.at[lax.rem(fx + step, FFN)], recv_f.at[fx], 11, number_f[step])
+        recv_f[fx] = send_f[fx]
 
     with jax.named_scope("last_wait"):
         settle(send_a.at[pl.ds(0, CTX - 1)], send_sem.at[0])
@@ -459,8 +464,8 @@
         settle(recv_e.at[0, pl.ds(0, SIDE - 1)], send_sem.at[13])
         settle(send_f.at[pl.ds(0, FFN - 1)], send_sem.at[11])
 
-        kept.wait()
-        settle(out.at[pl.ds(0, FFN - 1)], recv_sem.at[11])
+        settle(recv_f.at[pl.ds(0, FFN - 1)], recv_sem.at[11])
+        out[...] = jnp.sum(recv_f[...].astype(F32), axis=0).astype(BF16)
 
 
 def local(
@@ -468,9 +473,9 @@
     gate_proj, up_proj, down_proj, expert_ids, route_weight,
 ):
     anywhere = pl.BlockSpec(memory_space=pl.ANY)
-    parts = pl.pallas_call(
+    return pl.pallas_call(
         kernel,
-        out_shape=pltpu.VMEM((FFN, R, COLS), BF16),
+        out_shape=pltpu.VMEM((R, COLS), BF16),
         in_specs=[anywhere] * 12,
         out_specs=pl.BlockSpec(memory_space=pltpu.VMEM),
         scratch_shapes=[
@@ -501,6 +506,7 @@
             pltpu.VMEM((GROUPS, SIDE, 2 * SLOTS, QUARTER), BF16),
             pltpu.VMEM((SIDE, SIDE, GROUPS, SLOTS, QUARTER), BF16),
             pltpu.VMEM((FFN, R, COLS), BF16),
+            pltpu.VMEM((FFN, R, COLS), BF16),
             pltpu.VMEM((128, 128), BF16),
             pltpu.VMEM((128, 128), BF16),
             pltpu.VMEM((E_LOC, SLOTS, COLS), BF16),
@@ -524,7 +530,6 @@
         lengths, residual, norm_gain.reshape(1, COLS), expert_ids, route_weight,
         queries, key_cache, value_cache, o_weight, gate_proj, up_proj, down_proj,
     )
-    return jnp.sum(parts.astype(F32), axis=0).astype(BF16)
 
 
 def solution(mesh):

time: 46 us -> 46 us (level)
  other arithmetic: 0.61 us -> 0 us
  local copies, waits for them, and re-layouts: 0 us -> 0.6 us
    reduce_sum x1 -> x0, other arithmetic: 0.61 us -> none  [local(): return jnp.sum(parts.astype(F32), axis=0).astype(BF16)]
    unnamed x0 -> x1, local copies, waits for them, and re-layouts: none -> 0.6 us
where the time goes in v5:
time: 46 us; the launch traced here: 45.9 us
  Pallas kernels  45.3 us (98%)
  local copies, waits for them, and re-layouts  0.6 us (1%)
    pallas_call x1, Pallas kernels, local(): pl.pallas_call(kernel, out_shape=pltpu.VMEM((R, COLS), BF16), in_specs=[a...  45.3 us

profile of v5, /device:TPU:1, one launch (start us, length us, event | category | flops | bytes accessed | tf_op | source)
XLA Modules:
  0.0 45.9 jit_solution(13625324459355175245)
XLA Ops:
  0.0 45.3 %shard_map.118 = bf16[8,256]{1,0:T(8,128)(2,1)S(1)} custom-call(s32[8]{0:T(128)} %len_hbm.1, bf16[8,256]{1,0:T(8,128)(2,1)} %res_hbm.1, f32[1,256]{1,0:T(1,128)} %bitcast.1, s32[8,8]{1,0:T(8,128)} %ids_hbm.1, f32[8,8]{1,0:T(8,128)} %route_hbm.1, bf16[8,8192]{1,0:T(8,128)(2,1)} %q_hbm.1, bf16[8,128,512]{2,1,0:T(8,128)(2,1)} %k_hbm.1, ...), custom_call_target="tpu_custom_call" | custom-call | flops 1000000000 | bytes 26000000 | tf_op jit(solution)/shard_map/pallas_call | solution.py:476
  45.3 0.6 %copy.14 = bf16[8,256]{1,0:T(8,128)(2,1)} copy(bf16[8,256]{1,0:T(8,128)(2,1)S(1)} %shard_map.118) | data formatting | bytes 8192

commit v6 on v4

--- a/solution.py
+++ b/solution.py
@@ -322,13 +322,18 @@
             both = jnp.dot(rows[e], gu_v[e], preferred_element_type=F32)
             return both[:, 0:FFH], both[:, FFH:]
 
+        def half_of(g, step, span):
+            e = g * PER + turn(g, step)
+            return jnp.dot(rows[e], gu_v[e, :, span], preferred_element_type=F32).astype(BF16)
+
     with jax.named_scope("gate_up"):
         for g in range(GROUPS):
-            gate, upward = gate_up(g, 2)
-            send_1[g, 4] = gate.astype(BF16)
-            send_1[g, 5] = upward.astype(BF16)
+            send_1[g, 5] = half_of(g, 2, slice(FFH, 2 * FFH))
         for g in range(GROUPS):
             push(send_1.at[g, 5], passing.at[g], 9 + g, first_line(g, 3))
+        for g in range(GROUPS):
+            send_1[g, 4] = half_of(g, 2, slice(0, FFH))
+        for g in range(GROUPS):
             push(send_1.at[g, 4], recv_1.at[g, 4], 4 + g, first_line(g, 2))
         for g in range(GROUPS):
             gate, upward = gate_up(g, 1)
@@ -339,13 +344,13 @@
         for g in range(GROUPS):
             push(send_1.at[g, pl.ds(0, 2)], recv_1.at[g, pl.ds(0, 2)], 4 + g, first_line(g, 1))
             push(send_1.at[g, 2], recv_1.at[g, 2], 4 + g, first_line(g, 3))
-        for g in range(GROUPS):
-            own_1[g, 0], own_1[g, 1] = gate_up(g, 0)
         share_squares()
         for g in range(GROUPS):
             settle(passing.at[g], recv_sem.at[9 + g])
             send_1[g, 3] = (behind[g] + passing[g].astype(F32)).astype(BF16)
             push(send_1.at[g, 3], recv_1.at[g, 3], 4 + g, first_line(g, 3))
+        for g in range(GROUPS):
+            own_1[g, 0], own_1[g, 1] = gate_up(g, 0)
 
     with jax.named_scope("square_sums"):
         settle(recv_s.at[0, pl.ds(0, SIDE - 1)], recv_sem.at[6])

time: 46 us -> 45.9 us (level)
  no operation moved by 1% of the time
where the time goes in v6:
time: 45.9 us; the launch traced here: 45.8 us
  Pallas kernels  45.2 us (98%)
  other arithmetic  0.61 us (1%)
    pallas_call x1, Pallas kernels, local(): pl.pallas_call(kernel, out_shape=pltpu.VMEM((FFN, R, COLS), BF16), in_spe...  45.2 us

profile of v6, /device:TPU:1, one launch (start us, length us, event | category | flops | bytes accessed | tf_op | source)
XLA Modules:
  0.0 45.8 jit_solution(11682337394182957037)
XLA Ops:
  0.0 45.2 %shard_map.118 = bf16[8,8,256]{2,1,0:T(8,128)(2,1)S(1)} custom-call(s32[8]{0:T(128)} %len_hbm.1, bf16[8,256]{1,0:T(8,128)(2,1)} %res_hbm.1, f32[1,256]{1,0:T(1,128)} %bitcast.1, s32[8,8]{1,0:T(8,128)} %ids_hbm.1, f32[8,8]{1,0:T(8,128)} %route_hbm.1, bf16[8,8192]{1,0:T(8,128)(2,1)} %q_hbm.1, bf16[8,128,512]{2,1,0:T(8,128)(2,1)} %k_hbm.1, ...), custom_call_target="tpu_custom_call" | custom-call | flops 1000000000 | bytes 26000000 | tf_op jit(solution)/shard_map/pallas_call | solution.py:476
  45.2 0.6 %reduce_sum.12 = bf16[8,256]{1,0:T(8,128)(2,1)} reduce(bf16[8,8,256]{2,1,0:T(8,128)(2,1)S(1)} %shard_map.118, bf16[]{:T(256)} %constant.2.clone.1), dimensions={0}, to_apply=%region_0.0 | reduce | flops 14336 | bytes 36866 | tf_op jit(solution)/shard_map/reduce_sum | solution.py:532

commit v7 on v4

--- a/solution.py
+++ b/solution.py
@@ -95,8 +95,7 @@
             (ids_hbm, ids), (route_hbm, route), (res_hbm, residual), (gain_hbm, gain),
         ]
         first = [pltpu.make_async_copy(src, dst, in_sem.at[n]) for n, (src, dst) in enumerate(pairs)]
-        for copy in first[:4]:
-            copy.start()
+        first[0].start()
         kv_copies = []
         for m, (src, dst) in enumerate(((k_hbm, k_v), (v_hbm, v_v))):
             for n in range(2):
@@ -106,11 +105,11 @@
                 )
         for copy in kv_copies:
             copy.start()
-        for copy in first[4:]:
-            copy.start()
         for dx, dz in FAR_FIRST:
             greet(number_x[dx] + number_z[dz])
         every_ffn(greet)
+        for copy in first[1:]:
+            copy.start()
         o_copies = [
             pltpu.make_async_copy(
                 o_hbm.at[pl.ds(n * 128, 128)], o_v.at[pl.ds(n * 128, 128)], o_sem.at[n]
@@ -136,15 +135,6 @@
         row_r = lax.broadcasted_iota(jnp.int32, (128, 128), 0) & 7
         lane_full = lax.broadcasted_iota(jnp.int32, (1, 4, R, 128), 3)
         head4 = lax.broadcasted_iota(jnp.int32, (1, 4, R, 128), 1)
-        first[2].wait()
-        first[3].wait()
-        table = jnp.zeros((R, 128), F32)
-        ids_f = ids[...].astype(F32)
-        route_f = route[...]
-        for k in range(8):
-            table = jnp.where(lane8 == k, ids_f[:, k : k + 1], table)
-            table = jnp.where(lane8 == 8 + k, route_f[:, k : k + 1], table)
-        recv_r[fx] = table
         first[1].wait()
         for r in range(R):
             filled = jnp.where(sub8 == r, lengths[r], filled)
@@ -193,6 +183,15 @@
         kv_copies[0].wait()
         kv_copies[1].wait()
         flats = [weigh_up(k) for k in range(KVH)]
+        first[2].wait()
+        first[3].wait()
+        table = jnp.zeros((R, 128), F32)
+        ids_f = ids[...].astype(F32)
+        route_f = route[...]
+        for k in range(8):
+            table = jnp.where(lane8 == k, ids_f[:, k : k + 1], table)
+            table = jnp.where(lane8 == 8 + k, route_f[:, k : k + 1], table)
+        recv_r[fx] = table
         kv_copies[2].wait()
         kv_copies[3].wait()
         for copy in o_copies:

time: 46 us -> 46 us (level)
  no operation moved by 1% of the time
where the time goes in v7:
time: 46 us; the launch traced here: 45.9 us
  Pallas kernels  45.3 us (98%)
  other arithmetic  0.61 us (1%)
    pallas_call x1, Pallas kernels, local(): pl.pallas_call(kernel, out_shape=pltpu.VMEM((FFN, R, COLS), BF16), in_spe...  45.3 us

profile of v7, /device:TPU:1, one launch (start us, length us, event | category | flops | bytes accessed | tf_op | source)
XLA Modules:
  0.0 45.9 jit_solution(13846946834175922121)
XLA Ops:
  0.0 45.3 %shard_map.118 = bf16[8,8,256]{2,1,0:T(8,128)(2,1)S(1)} custom-call(s32[8]{0:T(128)} %len_hbm.1, bf16[8,256]{1,0:T(8,128)(2,1)} %res_hbm.1, f32[1,256]{1,0:T(1,128)} %bitcast.1, s32[8,8]{1,0:T(8,128)} %ids_hbm.1, f32[8,8]{1,0:T(8,128)} %route_hbm.1, bf16[8,8192]{1,0:T(8,128)(2,1)} %q_hbm.1, bf16[8,128,512]{2,1,0:T(8,128)(2,1)} %k_hbm.1, ...), custom_call_target="tpu_custom_call" | custom-call | flops 1000000000 | bytes 26000000 | tf_op jit(solution)/shard_map/pallas_call | solution.py:470
  45.3 0.6 %reduce_sum.12 = bf16[8,256]{1,0:T(8,128)(2,1)} reduce(bf16[8,8,256]{2,1,0:T(8,128)(2,1)S(1)} %shard_map.118, bf16[]{:T(256)} %constant.2.clone.1), dimensions={0}, to_apply=%region_0.0 | reduce | flops 14336 | bytes 36866 | tf_op jit(solution)/shard_map/reduce_sum | solution.py:526

commit v8 on v4

--- a/solution.py
+++ b/solution.py
@@ -42,7 +42,7 @@
     lengths, residual, gain, ids, route,
     q_v, k_v, v_v, o_v, gu_v, d_v,
     send_a, recv_a, send_b, recv_b, recv_c, recv_r, recv_s,
-    send_1, passing, behind, own_1, recv_1, send_2, recv_2, recv_e, send_f,
+    send_1, passing, behind, ahead, own_1, recv_1, send_2, recv_2, recv_e, send_f,
     pick, weigh, rows, results, partly,
     in_sem, kv_sem, o_sem, w_sem, send_sem, recv_sem, line_recv,
 ):
@@ -263,8 +263,8 @@
     with jax.named_scope("projection"):
         projected = jnp.dot(attended, o_v[...], preferred_element_type=F32)
         for c in range(CTX):
-            ahead, rest = projected[:, c * 256 : c * 256 + 128], projected[:, c * 256 + 128 : c * 256 + 256]
-            send_b[c] = jnp.concatenate([ahead, rest], axis=0).astype(BF16)
+            first_half, rest = projected[:, c * 256 : c * 256 + 128], projected[:, c * 256 + 128 : c * 256 + 256]
+            send_b[c] = jnp.concatenate([first_half, rest], axis=0).astype(BF16)
         for step in BLOCKS:
             for z in OTHERS + ((0,) if step else ()):
                 to = turn_x[step] * SIDE + turn_z[z]
@@ -328,24 +328,25 @@
             send_1[g, 4] = gate.astype(BF16)
             send_1[g, 5] = upward.astype(BF16)
         for g in range(GROUPS):
-            push(send_1.at[g, 5], passing.at[g], 9 + g, first_line(g, 3))
-            push(send_1.at[g, 4], recv_1.at[g, 4], 4 + g, first_line(g, 2))
-        for g in range(GROUPS):
-            gate, upward = gate_up(g, 1)
-            send_1[g, 0] = gate.astype(BF16)
+            push(send_1.at[g, 5], passing.at[g, 0], 9 + g, first_line(g, 3))
+            push(send_1.at[g, 4], passing.at[g, 1], 9 + g, first_line(g, 1))
+        for g in range(GROUPS):
+            ahead[g], upward = gate_up(g, 1)
             send_1[g, 1] = upward.astype(BF16)
             gate, behind[g] = gate_up(g, 3)
             send_1[g, 2] = gate.astype(BF16)
         for g in range(GROUPS):
-            push(send_1.at[g, pl.ds(0, 2)], recv_1.at[g, pl.ds(0, 2)], 4 + g, first_line(g, 1))
+            push(send_1.at[g, 1], recv_1.at[g, 1], 4 + g, first_line(g, 1))
             push(send_1.at[g, 2], recv_1.at[g, 2], 4 + g, first_line(g, 3))
         for g in range(GROUPS):
             own_1[g, 0], own_1[g, 1] = gate_up(g, 0)
         share_squares()
         for g in range(GROUPS):
             settle(passing.at[g], recv_sem.at[9 + g])
-            send_1[g, 3] = (behind[g] + passing[g].astype(F32)).astype(BF16)
+            send_1[g, 3] = (behind[g] + passing[g, 0].astype(F32)).astype(BF16)
+            send_1[g, 0] = (ahead[g] + passing[g, 1].astype(F32)).astype(BF16)
             push(send_1.at[g, 3], recv_1.at[g, 3], 4 + g, first_line(g, 3))
+            push(send_1.at[g, 0], recv_1.at[g, 0], 4 + g, first_line(g, 1))
 
     with jax.named_scope("square_sums"):
         settle(recv_s.at[0, pl.ds(0, SIDE - 1)], recv_sem.at[6])
@@ -359,7 +360,7 @@
             settle(recv_1.at[g], recv_sem.at[4 + g])
             gate = own_1[g, 0]
             upward = own_1[g, 1]
-            for c in (0, 2, 4):
+            for c in (0, 2):
                 gate = gate + recv_1[g, c].astype(F32)
             for c in (1, 3):
                 upward = upward + recv_1[g, c].astype(F32)
@@ -493,10 +494,11 @@
             pltpu.VMEM((FFN, R, 128), F32),
             pltpu.VMEM((2, SIDE, R, 128), F32),
             pltpu.VMEM((GROUPS, 6, SLOTS, FFH), BF16),
-            pltpu.VMEM((GROUPS, SLOTS, FFH), BF16),
+            pltpu.VMEM((GROUPS, 2, SLOTS, FFH), BF16),
+            pltpu.VMEM((GROUPS, SLOTS, FFH), F32),
             pltpu.VMEM((GROUPS, SLOTS, FFH), F32),
             pltpu.VMEM((GROUPS, 2, SLOTS, FFH), F32),
-            pltpu.VMEM((GROUPS, 5, SLOTS, FFH), BF16),
+            pltpu.VMEM((GROUPS, 4, SLOTS, FFH), BF16),
             pltpu.VMEM((GROUPS, SIDE, 2 * SLOTS, QUARTER), BF16),
             pltpu.VMEM((GROUPS, SIDE, 2 * SLOTS, QUARTER), BF16),
             pltpu.VMEM((SIDE, SIDE, GROUPS, SLOTS, QUARTER), BF16),

time: 46 us -> 45.8 us (level)
  no operation moved by 1% of the time
where the time goes in v8:
time: 45.8 us; the launch traced here: 45.7 us
  Pallas kernels  45 us (98%)
  other arithmetic  0.61 us (1%)
    pallas_call x1, Pallas kernels, local(): pl.pallas_call(kernel, out_shape=pltpu.VMEM((FFN, R, COLS), BF16), in_spe...  45 us

profile of v8, /device:TPU:1, one launch (start us, length us, event | category | flops | bytes accessed | tf_op | source)
XLA Modules:
  0.0 45.7 jit_solution(18129076929842661450)
XLA Ops:
  0.0 45.0 %shard_map.118 = bf16[8,8,256]{2,1,0:T(8,128)(2,1)S(1)} custom-call(s32[8]{0:T(128)} %len_hbm.1, bf16[8,256]{1,0:T(8,128)(2,1)} %res_hbm.1, f32[1,256]{1,0:T(1,128)} %bitcast.1, s32[8,8]{1,0:T(8,128)} %ids_hbm.1, f32[8,8]{1,0:T(8,128)} %route_hbm.1, bf16[8,8192]{1,0:T(8,128)(2,1)} %q_hbm.1, bf16[8,128,512]{2,1,0:T(8,128)(2,1)} %k_hbm.1, ...), custom_call_target="tpu_custom_call" | custom-call | flops 1000000000 | bytes 26000000 | tf_op jit(solution)/shard_map/pallas_call | solution.py:472
  45.1 0.6 %reduce_sum.12 = bf16[8,256]{1,0:T(8,128)(2,1)} reduce(bf16[8,8,256]{2,1,0:T(8,128)(2,1)S(1)} %shard_map.118, bf16[]{:T(256)} %constant.2.clone.1), dimensions={0}, to_apply=%region_0.0 | reduce | flops 14336 | bytes 36866 | tf_op jit(solution)/shard_map/reduce_sum | solution.py:529
